TPU v7x, 128 devices: a whole 4x4x4 slice. The times are simulated.
128 devices in a mesh: gx: 16 (over z, x), gy: 8 (over y, core).
Axes of the slice: x: 4, y: 4, z: 4, core: 2. Of those that a mesh axis runs over, the one named last changes fastest.
Arguments:
- volume: bfloat16 [512, 512, 2, 512], P('gx', 'gy'), may hold values from -6 to 6
- spectra: bfloat16 [128, 512, 2, 128], P(('gx', 'gy')), may hold values from -6 to 6
- weights: float32 [128, 512, 2], P(('gx', 'gy')), may hold values from 0.1 to 1
- owners: int32 [128, 512, 2], P(('gx', 'gy')), may hold values from 0 to 127, all different within a row; in each aligned block of 512 rows (0 to 511, 512 to 1023, ..., all dimensions but the last counted through in order) at most 20 rows name the same one
- block_ids: int32 [128, 512, 2], P(('gx', 'gy')), may hold values from 0 to 8191
- pose_ids: int32 [128], P(('gx', 'gy')), may hold values from 0 to 63
- class_ids: int32 [128], P(('gx', 'gy')), may hold values from 0 to 15
- pose_shift: float32 [64, 2], replicated, may hold values from -4 to 4
- defocus: float32 [16], replicated, may hold values from 20 to 200
Outputs:
- real_map: bfloat16 [512, 512, 2, 512], P(None, 'gx', None, 'gy')
- update: float32 [512, 512, 2, 512], P('gx', 'gy')
- misfit: float32 [128], P(('gx', 'gy'))
Inputs may be any that keep to these rules, and one draw needn't show every extreme that they name: Within the rows (particle, tile) of one device, each owner is named by at most 20 rows, and by exactly 20 rows in some device's rows; a row names two different owners.
All inputs are finite; a program needn't handle non-finite values.
Results may differ from a plain program's by a relative error of at most 0.008.
Values may be sent and summed in bfloat16 or wider, within the bound.
No kernel may reach another device: no remote copies, remote signals or barrier semaphores. Data moves between devices by JAX's collectives and lax.ppermute only.
A program may use at most 128 MiB of HBM per device.

v0:
```python
import math

import jax
import jax.numpy as jnp
import numpy as np
from jax import lax
from jax.experimental import pallas as pl
from jax.experimental.pallas import tpu as pltpu
from jax.sharding import PartitionSpec as P

BOX = 256
CAP = 20
CHUNKS = (16, 16)
BF = jnp.bfloat16
F32 = jnp.float32
I32 = jnp.int32
VMEM_BYTES = 52 * 1024 * 1024


def dft_tables(length, gx, gy):
    n = np.arange(length)
    angles = (n[:, None] * n[None, :] % length) * (2.0 * np.pi / length)
    cosine = (np.cos(angles) / math.sqrt(length)).astype(BF)
    sine = (np.sin(angles) / math.sqrt(length)).astype(BF)
    upper = np.concatenate([cosine, sine], axis=1)
    lower = np.concatenate([-sine, cosine], axis=1)
    full = np.concatenate([upper, lower], axis=0)
    third = (
        full.reshape(2 * length, 2, gy, length // gy)
        .transpose(0, 2, 1, 3)
        .reshape(2 * length, 2 * length)
    )
    second = np.concatenate([cosine, sine], axis=1)
    local_a = length // gx
    lines = np.arange(length).reshape(gx, local_a)
    starts = np.cumsum((0,) + CHUNKS)
    rows = np.concatenate(
        [lines[:, starts[j] : starts[j + 1]].reshape(-1) for j in range(len(CHUNKS))]
    )
    first = np.concatenate([cosine[rows], sine[rows]], axis=0)
    return third, second, first


def frequencies(tile_count, block_len):
    pixel = jnp.arange(tile_count * block_len, dtype=I32).reshape(tile_count, block_len)
    freq_x = pixel % BOX
    freq_y = pixel // BOX
    freq_x = jnp.where(freq_x >= BOX // 2, freq_x - BOX, freq_x).astype(F32)
    freq_y = jnp.where(freq_y >= BOX // 2, freq_y - BOX, freq_y).astype(F32)
    radius_sq = (freq_x * freq_x + freq_y * freq_y) / (BOX * BOX / 4.0)
    return (freq_x, freq_y, radius_sq)


def params(**more):
    return pltpu.CompilerParams(vmem_limit_bytes=VMEM_BYTES, **more)


def near(x):
    return pltpu.with_memory_space_constraint(x, pltpu.VMEM)


def iota(shape, dim):
    return lax.broadcasted_iota(I32, shape, dim)


def dot(a, b):
    return jnp.dot(a, b, preferred_element_type=F32)


def shifted_index(iy, k, gy, direction):
    chips = gy // 2
    return ((iy // 2 + chips + direction * (k // 2)) % chips) * 2 + (iy % 2 + k % 2) % 2


def slots_kernel(own_ref, bid_ref, sent_ref, row_ref, col_ref):
    peers = sent_ref.shape[0]
    own = jnp.concatenate([own_ref[0:1, :], own_ref[1:2, :]], axis=1)
    bid = jnp.concatenate([bid_ref[0:1, :], bid_ref[1:2, :]], axis=1)
    count = own.shape[1]
    match = iota((peers, count), 0) == own
    hot = jnp.where(match, 1.0, 0.0).astype(F32)
    before = jnp.where(iota((count, count), 0) < iota((count, count), 1), 1.0, 0.0).astype(BF)
    prefix = dot(hot.astype(BF), before)
    slot = jnp.sum(hot * prefix, axis=0, keepdims=True)
    slot_i = slot.astype(I32)
    here = iota((peers, count), 0) == slot_i
    high = jnp.where(here, ((bid >> 6) + 1).astype(F32), 0.0).astype(BF)
    low = jnp.where(here, (bid & 63).astype(F32), 0.0).astype(BF)
    nt = (((1,), (1,)), ((), ()))
    hot_b = hot.astype(BF)
    high_at = lax.dot_general(hot_b, high, nt, preferred_element_type=F32)
    low_at = lax.dot_general(hot_b, low, nt, preferred_element_type=F32)
    sent_ref[...] = (high_at * 64.0 + low_at - 64.0).astype(I32)
    target = own * CAP + slot_i
    row_ref[...] = target
    wide = jnp.broadcast_to(target.astype(F32), (peers, count))
    col_ref[...] = wide.T.astype(I32)


def lookup_kernel(ids_ref, vol_ref, out_ref, tmp_ref):
    def peer(p, carry):
        at = pl.multiple_of(p * (2 * CAP), 8)
        for s in range(CAP):
            block = jnp.maximum(ids_ref[p, s], 0)
            tmp_ref[pl.ds(at + 2 * s, 2), :] = vol_ref[pl.ds(pl.multiple_of(2 * block, 2), 2), :]
        return carry

    lax.fori_loop(0, ids_ref.shape[0], peer, 0)
    out_ref[...] = tmp_ref[...].astype(BF)


def parts_kernel(part_ref, out_ref):
    wide = jnp.broadcast_to(part_ref[...].astype(F32), (out_ref.shape[1], out_ref.shape[0]))
    out_ref[...] = wide.T.astype(I32)


def split_parts(rows_ref, tmp_ref):
    tmp_ref[...] = rows_ref[...].astype(F32)
    count = tmp_ref.shape[0] // 2
    return tmp_ref[pl.ds(0, count, stride=2), :], tmp_ref[pl.ds(1, count, stride=2), :]


def particle_kernel(ret_ref, col_ref, row_ref, w_ref, shift_ref, ctf_ref, out_ref, mis_ref, tmp_ref):
    total = ret_ref.shape[0] // 2
    tiles = w_ref.shape[0]
    lanes = iota((2 * tiles, 128), 1)
    col = col_ref[...]
    real, imag = split_parts(ret_ref, tmp_ref)
    blocks = jnp.concatenate([real, imag], axis=1).astype(BF)
    pick = jnp.concatenate(
        [jnp.where(col == lanes + 128 * b, 1.0, 0.0).astype(BF) for b in range(total // 128)], axis=1
    )
    fetched = dot(pick, blocks)
    w0 = w_ref[:, 0:1]
    w1 = w_ref[:, 1:2]
    projected = w0 * fetched[:tiles] + w1 * fetched[tiles:]
    ctf = ctf_ref[...]
    ctf2 = jnp.concatenate([ctf, ctf], axis=1)
    residual = shift_ref[...] - ctf2 * projected
    mis_ref[...] = jnp.sum(residual * residual, axis=0, keepdims=True)
    both = jnp.concatenate(
        [((w0 * ctf2) * residual).astype(BF), ((w1 * ctf2) * residual).astype(BF)], axis=0
    )
    row = row_ref[...]
    step = 512
    for b in range(total // step):
        put = jnp.where(iota((step, 2 * tiles), 0) + step * b == row, 1.0, 0.0).astype(BF)
        result = dot(put, both)
        for r in range(2):
            tmp_ref[pl.ds(2 * b * step + r, step, stride=2), :] = result[:, r * 128 : (r + 1) * 128]
    out_ref[...] = tmp_ref[...].astype(BF)


def insert_lines(first_line, inc_ref, line_ref, part_ref, vol_ref, table_ref, upd_ref, tmp_ref, exp_ref):
    total = exp_ref.shape[0]
    lines = vol_ref.shape[0]

    @pl.when(pl.program_id(0) == 0)
    def _():
        part = part_ref[...]
        for r, inc in enumerate(split_parts(inc_ref, tmp_ref)):
            for m in range(4):
                exp_ref[:, (r * 4 + m) * 128 : (r * 4 + m + 1) * 128] = jnp.where(part == m, inc, 0.0).astype(BF)

    base = first_line + pl.program_id(0) * lines
    pick = jnp.where(iota((lines, total), 0) + base == line_ref[...], 1.0, 0.0).astype(BF)
    update = dot(pick, exp_ref[...])
    upd_ref[...] = update
    inserted = (vol_ref[...].astype(F32) + update).astype(BF)
    return dot(inserted, table_ref[...])


def insert_first(inc_ref, line_ref, part_ref, vol_ref, table_ref, upd_ref, out_ref, tmp_ref, exp_ref):
    passed = insert_lines(0, inc_ref, line_ref, part_ref, vol_ref, table_ref, upd_ref, tmp_ref, exp_ref)
    for d in range(out_ref.shape[0]):
        out_ref[d] = passed[:, d * 128 : (d + 1) * 128].astype(BF)


def insert_next(first_line, iy_ref, inc_ref, line_ref, part_ref, vol_ref, table_ref, old_ref, upd_ref, *refs):
    outs = refs[:-3]
    tmp_ref, exp_ref, pass_ref = refs[-3:]
    passed = insert_lines(first_line, inc_ref, line_ref, part_ref, vol_ref, table_ref, upd_ref, tmp_ref, exp_ref)
    pass_ref[...] = passed.astype(BF)
    for k, out_ref in enumerate(outs):
        dest = shifted_index(iy_ref[0], k, len(outs), 1)
        out_ref[...] = pass_ref[:, pl.ds(pl.multiple_of(dest * 128, 128), 128)]


def second_lines(x, a, count, table_ref, tmp_ref):
    length, lanes = x.shape[0], x.shape[1] // 2
    sign = jnp.where(iota((1, 2 * lanes), 1) % lanes < lanes // 2, -1.0, 1.0).astype(F32)
    t0 = pltpu.roll(x[:, :lanes].astype(F32), lanes // 2, 1)
    t1 = pltpu.roll(x[:, lanes:].astype(F32), lanes // 2, 1)
    turned = (jnp.concatenate([t0, t1], axis=1) * sign).astype(BF)
    y = dot(table_ref[...], jnp.concatenate([x, turned], axis=0))
    tmp_ref[pl.ds(a, length, stride=count), :] = y[:, :lanes]
    tmp_ref[pl.ds(a + 1, length, stride=count), :] = y[:, lanes:]


def second_first(in_ref, table_ref, out_ref, tmp_ref):
    peers, count, rows, lanes = in_ref.shape
    length = peers * rows
    for a in range(0, count, 2):
        x = jnp.concatenate([in_ref[:, a + i].reshape(length, lanes) for i in range(2)], axis=1)
        second_lines(x, a, count, table_ref, tmp_ref)
    out_ref[...] = tmp_ref[...].astype(BF)


def second_next(iy_ref, *refs):
    ins = refs[:-4]
    table_ref, out_ref, tmp_ref, x_ref = refs[-4:]
    count, rows, lanes = ins[0].shape
    for a in range(0, count, 2):
        for k, ref in enumerate(ins):
            source = shifted_index(iy_ref[0], k, len(ins), -1)
            at = pl.ds(pl.multiple_of(source * rows, rows), rows)
            for i in range(2):
                x_ref[a // 2, at, i * lanes : (i + 1) * lanes] = ref[a + i]
    for a in range(0, count, 2):
        second_lines(x_ref[a // 2], a, count, table_ref, tmp_ref)
    out_ref[...] = tmp_ref[...].astype(BF)


def turn_rows(ref, b):
    x = ref[:, b]
    return x.reshape(x.shape[0] * x.shape[1], x.shape[2]).astype(F32).T


def turn_kernel(in_ref, out_ref):
    for b in range(in_ref.shape[1]):
        out_ref[b] = turn_rows(in_ref, b).astype(BF)


def first_kernel(*refs):
    *early_refs, late_ref, table_ref, out_ref = refs
    group = out_ref.shape[0]
    half = out_ref.shape[2]
    rows = []
    for b in range(group):
        late = turn_rows(late_ref, b).astype(BF)
        x = jnp.concatenate([ref[b] for ref in early_refs] + [late], axis=1)
        rows.append(jnp.concatenate([x, jnp.concatenate([-x[half:], x[:half]], axis=0)], axis=1))
    y = dot(jnp.concatenate(rows, axis=0), table_ref[...])
    for b in range(group):
        for s in range(2):
            at = (2 * b + s) * half
            out_ref[b, s] = y[at : at + half].astype(BF)


def local(volume, spectra, weights, owners, block_ids, pose_ids, class_ids, pose_shift, defocus):
    gx = lax.axis_size("gx")
    gy = lax.axis_size("gy")
    peers = gx * gy
    local_a, local_b, _, length = volume.shape
    tiles = spectra.shape[1]
    block_len = spectra.shape[3]
    lines = local_a * local_b
    total = peers * CAP
    rows = 2 * total
    refs = 2 * tiles
    third, second, first = dft_tables(length, gx, gy)
    whole = pl.BlockSpec(memory_space=pltpu.VMEM)

    own = owners.transpose(0, 2, 1).reshape(2, tiles)
    bid = block_ids.transpose(0, 2, 1).reshape(2, tiles)
    sent, row, col = pl.pallas_call(
        slots_kernel,
        out_shape=(
            jax.ShapeDtypeStruct((peers, 128), I32),
            jax.ShapeDtypeStruct((1, refs), I32),
            jax.ShapeDtypeStruct((refs, 128), I32),
        ),
        in_specs=[whole] * 2,
        out_specs=(whole,) * 3,
        compiler_params=params(),
        name="slots",
    )(own, bid)
    got = lax.all_to_all(
        sent.reshape(peers, 1, 128), ("gx", "gy"), split_axis=0, concat_axis=0, tiled=True
    ).reshape(peers, 128)

    scalars = pl.BlockSpec(memory_space=pltpu.SMEM)
    vol = volume.reshape(lines, 2 * length)
    per_line = length // block_len
    vol_rows = (
        volume.astype(F32)
        .reshape(lines, 2, per_line, block_len)
        .transpose(0, 2, 1, 3)
        .reshape(lines * per_line * 2, block_len)
    )
    looked = pl.pallas_call(
        lookup_kernel,
        out_shape=jax.ShapeDtypeStruct((rows, block_len), BF),
        in_specs=[scalars, whole],
        out_specs=whole,
        scratch_shapes=[pltpu.VMEM((rows, block_len), F32)],
        compiler_params=params(),
        name="lookup",
    )(got, vol_rows)
    returned = lax.all_to_all(
        looked.reshape(peers, 2 * CAP, block_len), ("gx", "gy"), split_axis=0, concat_axis=0, tiled=True
    ).reshape(rows, block_len)

    class_match = class_ids[:, None] == jnp.arange(defocus.shape[0], dtype=I32)[None, :]
    defocus_part = jnp.sum(jnp.where(class_match, defocus[None, :], 0.0), axis=1)
    pose_match = pose_ids[:, None, None] == jnp.arange(pose_shift.shape[0], dtype=I32)[None, :, None]
    shift_xy = jnp.sum(jnp.where(pose_match, pose_shift[None, :, :], 0.0), axis=1)
    freq_x, freq_y, radius_sq = frequencies(tiles, block_len)
    phase = -2.0 * math.pi / BOX * (freq_x * shift_xy[0, 0] + freq_y * shift_xy[0, 1])
    cosine = jnp.cos(phase)
    sine = jnp.sin(phase)
    spec_re = spectra[0, :, 0, :].astype(F32)
    spec_im = spectra[0, :, 1, :].astype(F32)
    shifted = jnp.concatenate([spec_re * cosine - spec_im * sine, spec_re * sine + spec_im * cosine], axis=1)
    ctf = -jnp.sin(defocus_part[0] * radius_sq + 0.1)

    ids = jnp.maximum(got[:, :CAP].reshape(1, total), -4)
    line_row = ids >> 2
    part_row = ids & 3
    weight = weights.reshape(tiles, 2)
    returned, line_row, part_row, weight, shifted, ctf = lax.optimization_barrier(
        (returned, line_row, part_row, weight, shifted, ctf)
    )
    part_col = pl.pallas_call(
        parts_kernel,
        out_shape=jax.ShapeDtypeStruct((total, 128), I32),
        in_specs=[whole],
        out_specs=whole,
        compiler_params=params(),
        cost_estimate=pl.CostEstimate(flops=1 << 22, bytes_accessed=1 << 22, transcendentals=0),
        name="parts",
    )(part_row)

    outgoing, squares = pl.pallas_call(
        particle_kernel,
        out_shape=(
            jax.ShapeDtypeStruct((rows, block_len), BF),
            jax.ShapeDtypeStruct((1, 2 * block_len), F32),
        ),
        in_specs=[whole] * 6,
        out_specs=(whole,) * 2,
        scratch_shapes=[pltpu.VMEM((rows, block_len), F32)],
        compiler_params=params(),
        name="particle",
    )(near(returned), col, row, weight, shifted, ctf)
    incoming = lax.all_to_all(
        outgoing.reshape(peers, 2 * CAP, block_len), ("gx", "gy"), split_axis=0, concat_axis=0, tiled=True
    ).reshape(rows, block_len)
    misfit = (jnp.sum(squares) / (2.0 * tiles * block_len)).reshape(1)
    incoming, part_col = lax.optimization_barrier((incoming, part_col))

    iy = lax.axis_index("gy").astype(I32).reshape(1)
    step = 256
    insert_scratch = [pltpu.VMEM((rows, block_len), F32), pltpu.VMEM((total, 2 * length), BF)]
    update_shape = jax.ShapeDtypeStruct((lines, 2 * length), F32)

    def second_shapes(count):
        return {
            "out_shape": jax.ShapeDtypeStruct((length * count, 128), BF),
            "out_specs": whole,
            "compiler_params": params(),
        }

    def cross(x, count):
        x = x.reshape(gx, (length // gx) * count, 128)
        return lax.all_to_all(x, "gx", split_axis=0, concat_axis=0, tiled=True).reshape(
            gx, length // gx, count, 128
        )

    crossed = []
    before = None
    start = 0
    for j, count in enumerate(CHUNKS):
        chunk_lines = count * local_b
        steps = chunk_lines // step
        skip = start * local_b // step
        block = pl.BlockSpec((step, 2 * length), lambda i, skip=skip: (i + skip, 0))
        if j == 0:
            update, out = pl.pallas_call(
                insert_first,
                grid=(steps,),
                out_shape=(update_shape, jax.ShapeDtypeStruct((gy, chunk_lines, 128), BF)),
                in_specs=[whole] * 3 + [block, whole],
                out_specs=(block, pl.BlockSpec((gy, step, 128), lambda i: (0, i, 0))),
                scratch_shapes=insert_scratch,
                compiler_params=params(dimension_semantics=("arbitrary",)),
                name="insert0",
            )(near(incoming), line_row, near(part_col), vol, third)
            arrived = lax.all_to_all(out, "gy", split_axis=0, concat_axis=0, tiled=True)
        else:
            update, *pieces = pl.pallas_call(
                lambda *r, first_line=start * local_b: insert_next(first_line, *r),
                grid=(steps,),
                out_shape=(update_shape,) + (jax.ShapeDtypeStruct((chunk_lines, 128), BF),) * gy,
                in_specs=[scalars] + [whole] * 3 + [block, whole, pl.BlockSpec(memory_space=pl.ANY)],
                out_specs=(block,) + (pl.BlockSpec((step, 128), lambda i: (i, 0)),) * gy,
                scratch_shapes=insert_scratch + [pltpu.VMEM((step, 2 * length), BF)],
                input_output_aliases={6: 0},
                compiler_params=params(dimension_semantics=("arbitrary",)),
                name=f"insert{j}",
            )(iy, incoming, line_row, part_col, vol, third, update)
            before, pieces = lax.optimization_barrier((before, pieces))
            arrived = [pieces[0]]
            for k in range(1, gy):
                pairs = [(i, shifted_index(i, k, gy, 1)) for i in range(gy)]
                arrived.append(lax.ppermute(pieces[k], "gy", pairs))
        if before is not None:
            crossed.append((before, start - CHUNKS[j - 1], CHUNKS[j - 1]))
        before = arrived
        start += count
    crossed.append((before, start - CHUNKS[-1], CHUNKS[-1]))

    for j, (arrived, start, count) in enumerate(crossed):
        tmp = pltpu.VMEM((length * count, 128), F32)
        if j == 0:
            done = pl.pallas_call(
                second_first,
                in_specs=[whole] * 2,
                scratch_shapes=[tmp],
                name="second0",
                **second_shapes(count),
            )(near(arrived.reshape(gy, count, local_b, 128)), second)
        else:
            done = pl.pallas_call(
                second_next,
                in_specs=[scalars] + [whole] * (gy + 1),
                scratch_shapes=[tmp, pltpu.VMEM((count // 2, length, 256), BF)],
                name=f"second{j}",
                **second_shapes(count),
            )(iy, *[x.reshape(count, local_b, 128) for x in arrived], second)
        crossed[j] = cross(done, count)

    out_b = length // gx
    out_c = length // gy
    group = 8

    def rows_spec(count):
        return pl.BlockSpec((gx, group, count, 128), lambda i: (0, i, 0, 0))

    def turned_spec(count):
        return pl.BlockSpec((group, 128, gx * count), lambda i: (i, 0, 0))

    turned = [
        pl.pallas_call(
            turn_kernel,
            grid=(out_b // group,),
            out_shape=jax.ShapeDtypeStruct((out_b, 128, gx * count), BF),
            in_specs=[rows_spec(count)],
            out_specs=turned_spec(count),
            compiler_params=params(dimension_semantics=("arbitrary",)),
            name=f"turn{j}",
        )(crossed[j])
        for j, count in enumerate(CHUNKS[:-1])
    ]
    real_map = pl.pallas_call(
        first_kernel,
        grid=(out_b // group,),
        out_shape=jax.ShapeDtypeStruct((out_b, 2, out_c, length), BF),
        in_specs=[turned_spec(count) for count in CHUNKS[:-1]] + [rows_spec(CHUNKS[-1]), whole],
        out_specs=pl.BlockSpec((group, 2, out_c, length), lambda i: (i, 0, 0, 0)),
        compiler_params=params(dimension_semantics=("arbitrary",)),
        name="first",
    )(*turned, crossed[-1], first)
    update = update.reshape(local_a, local_b, 2, length)
    return (real_map.transpose(3, 0, 1, 2), update, misfit)


def solution(mesh):
    in_specs = (
        P("gx", "gy", None, None),
        P(("gx", "gy"), None, None, None),
        P(("gx", "gy"), None, None),
        P(("gx", "gy"), None, None),
        P(("gx", "gy"), None, None),
        P(("gx", "gy")),
        P(("gx", "gy")),
        P(),
        P(),
    )
    out_specs = (P(None, "gx", None, "gy"), P("gx", "gy", None, None), P(("gx", "gy")))
    return jax.shard_map(local, mesh=mesh, in_specs=in_specs, out_specs=out_specs, check_vma=False)
```

profile of v0, /device:TPU:0, one launch (start us, length us, event | category | flops | bytes accessed | tf_op | source)
XLA Modules:
  0.0 240.4 jit_solution(3117953126690168232)
XLA Ops:
  0.6 0.7 copy-done.5
  1.3 0.7 copy-done.6
  2.0 1.4 slots.1
  3.4 0.8 copy-done.3
  4.2 11.1 %all-to-all-start = ((s32[128,1,128]{2,1,0:T(1,128)}), s32[128,1,128]{2,1,0:T(1,128)S(1)}, u32[]{:S(2)}, u32[]{:S(2)}) async-start(s32[128,1,128]{2,1,0:T(1,128)} %bitcast.5), calls=%async_computation | async-start | bytes 131072 | tf_op jit(solution)/shard_map/all_to_all | solution.py:278
  16.0 6.6 %convert.7 = f32[2048,2,4,128]{3,1,2,0:T(2,128)} convert(bf16[2048,2,4,128]{3,1,2,0:T(2,128)(2,1)} %bitcast.79) | non-fusion elementwise | flops 2097152 | bytes 12582912 | tf_op jit(solution)/shard_map/reshape | solution.py:289
  22.6 2.0 all-to-all-done
  24.5 9.3 %lookup.1 = bf16[5120,128]{1,0:T(8,128)(2,1)} custom-call(s32[128,128]{1,0:T(8,128)S(1)} %bitcast.65, f32[16384,128]{1,0:T(8,128)} %bitcast.78), custom_call_target="tpu_custom_call" | custom-call | tf_op jit(solution)/shard_map/lookup/pallas_call | solution.py:291
  33.9 7.8 %all-to-all-start.1 = ((bf16[128,40,128]{2,1,0:T(8,128)(2,1)}), bf16[128,40,128]{2,1,0:T(8,128)(2,1)S(1)}, u32[]{:S(2)}, u32[]{:S(2)}) async-start(bf16[128,40,128]{2,1,0:T(8,128)(2,1)} %bitcast.10), calls=%async_computation.1 | async-start | bytes 2621440 | tf_op jit(solution)/shard_map/all_to_all | solution.py:300
  41.6 0.6 fusion.11
  42.9 0.1 copy.26
  43.7 0.1 select_reduce_fusion
  43.9 0.6 fusion.13
  44.4 1.2 sine_negate_fusion.ctf_ref
  45.7 0.4 fusion.12
  46.0 2.6 %fusion = (f32[512,128]{1,0:T(8,128)S(1)}, f32[512,128]{1,0:T(8,128)S(1)}) fusion(f32[]{:T(128)} %bitcast.17, f32[]{:T(128)} %bitcast.16, bf16[1,512,1,128]{3,2,1,0:T(2,128)(2,1)S(1)} %get-tuple-element.72, bf16[1,512,1,128]{3,2,1,0:T(2,128)(2,1)S(1)} %get-tuple-element.71), kind=kLoop, calls=%fused_computation.12 | loop fusion | flops 2686976 | bytes 786440 | tf_op jit(solution)/shard_map/sub | solution.py:314
  48.7 0.8 pad_maximum_fusion.shift_ref
  49.5 0.1 and.34.part_ref
  49.7 0.7 shift_right_arithmetic.19.line_ref.r_2_
  50.4 13.2 %all-to-all-done.1 = bf16[128,40,128]{2,1,0:T(8,128)(2,1)S(1)} async-done(((bf16[128,40,128]{2,1,0:T(8,128)(2,1)}), bf16[128,40,128]{2,1,0:T(8,128)(2,1)S(1)}, u32[]{:S(2)}, u32[]{:S(2)}) %all-to-all-start.1) | async-done | bytes 1310752 | tf_op jit(solution)/shard_map/all_to_all | solution.py:300
  63.6 8.3 %particle.1 = (bf16[5120,128]{1,0:T(8,128)(2,1)}, f32[1,256]{1,0:T(1,128)S(1)}) custom-call(bf16[5120,128]{1,0:T(8,128)(2,1)S(1)} %bitcast.63, s32[1024,128]{1,0:T(8,128)} %copy-done.3, s32[1,1024]{1,0:T(1,128)S(1)} %get-tuple-element.39.row_ref, f32[512,2]{1,0:T(8,128)S(1)} %bitcast.64, f32[512,256]{1,0:T(8,128)} %pad_maximum_fusion.shift_ref, ...), custom_call_target="tpu_custom_call" | custom-call | tf_op jit(solution)/shard_map/particle/pallas_call | solution.py:334
  71.9 4.8 %all-to-all-start.2 = ((bf16[128,40,128]{2,1,0:T(8,128)(2,1)}), bf16[128,40,128]{2,1,0:T(8,128)(2,1)S(1)}, u32[]{:S(2)}, u32[]{:S(2)}) async-start(bf16[128,40,128]{2,1,0:T(8,128)(2,1)} %bitcast.85), calls=%async_computation.2 | async-start | bytes 2621440 | tf_op jit(solution)/shard_map/all_to_all | solution.py:346
  76.7 5.4 %copy.31 = bf16[256,8,2,512]{3,1,2,0:T(8,128)(2,1)} copy(bf16[256,8,2,512]{3,2,1,0:T(2,128)(2,1)} %bitcast.80) | data formatting | bytes 8388608
  82.1 0.4 parts.1.part_ref.r_3_
  82.5 15.9 %all-to-all-done.2 = bf16[128,40,128]{2,1,0:T(8,128)(2,1)S(1)} async-done(((bf16[128,40,128]{2,1,0:T(8,128)(2,1)}), bf16[128,40,128]{2,1,0:T(8,128)(2,1)S(1)}, u32[]{:S(2)}, u32[]{:S(2)}) %all-to-all-start.2) | async-done | bytes 1310752 | tf_op jit(solution)/shard_map/all_to_all | solution.py:346
  98.4 14.6 %insert0.1 = (f32[2048,1024]{1,0:T(8,128)}, bf16[8,1024,128]{2,1,0:T(8,128)(2,1)}) custom-call(bf16[5120,128]{1,0:T(8,128)(2,1)S(1)} %bitcast.60, s32[1,2560]{1,0:T(1,128)} %shift_right_arithmetic.19.line_ref.r_2_, s32[2560,128]{1,0:T(8,128)S(1)} %parts.1.part_ref.r_3_, bf16[2048,1024]{1,0:T(8,128)(2,1)} %bitcast.76, ...), custom_call_target="tpu_custom_call" | custom-call | tf_op jit(solution)/shard_map/insert0/pallas_call | solution.py:379
  113.0 3.6 %all-to-all-start.3 = ((bf16[8,1024,128]{2,1,0:T(8,128)(2,1)}), bf16[8,1024,128]{2,1,0:T(8,128)(2,1)S(1)}, u32[]{:S(2)}, u32[]{:S(2)}) async-start(bf16[8,1024,128]{2,1,0:T(8,128)(2,1)} %get-tuple-element.48), calls=%async_computation.3 | async-start | bytes 4194304 | tf_op jit(solution)/shard_map/all_to_all | solution.py:389
  116.7 15.2 %insert1.1 = (f32[2048,1024]{1,0:T(8,128)}, bf16[1024,128]{1,0:T(8,128)(2,1)S(1)}, bf16[1024,128]{1,0:T(8,128)(2,1)S(1)}, bf16[1024,128]{1,0:T(8,128)(2,1)S(1)},...) custom-call(s32[1]{0:T(128)} %bitcast.24.r_0_.iy_ref, ...), custom_call_target="tpu_custom_call", output_to_operand_aliasing={{0}: (6, {})} | custom-call | tf_op jit(solution)/shard_map/insert1/pallas_call | solution.py:391
  131.8 0.7 copy-done.7
  132.6 0.7 copy-done.9
  133.3 10.5 %all-to-all-done.3 = bf16[8,1024,128]{2,1,0:T(8,128)(2,1)S(1)} async-done(((bf16[8,1024,128]{2,1,0:T(8,128)(2,1)}), bf16[8,1024,128]{2,1,0:T(8,128)(2,1)S(1)}, u32[]{:S(2)}, u32[]{:S(2)}) %all-to-all-start.3) | async-done | bytes 2097184 | tf_op jit(solution)/shard_map/all_to_all | solution.py:389
  143.8 5.9 %second0.1 = bf16[8192,128]{1,0:T(8,128)(2,1)} custom-call(bf16[8,16,64,128]{3,2,1,0:T(8,128)(2,1)S(1)} %bitcast.62, bf16[512,1024]{1,0:T(8,128)(2,1)} %constant.64.clone.table_ref.refs_8_), custom_call_target="tpu_custom_call" | custom-call | tf_op jit(solution)/shard_map/second0/pallas_call | solution.py:416
  149.7 4.6 %all-to-all-start.4 = ((bf16[16,512,128]{2,1,0:T(8,128)(2,1)}), bf16[16,512,128]{2,1,0:T(8,128)(2,1)}, u32[]{:S(2)}, u32[]{:S(2)}) async-start(bf16[16,512,128]{2,1,0:T(8,128)(2,1)} %bitcast.81), calls=%async_computation.4 | async-start | bytes 4194304 | tf_op jit(solution)/shard_map/all_to_all | solution.py:366
  154.4 0.7 collective-permute-start.1
  155.1 3.8 %collective-permute-start.3 = (bf16[1024,128]{1,0:T(8,128)(2,1)S(1)}, bf16[1024,128]{1,0:T(8,128)(2,1)S(1)}, u32[]{:S(2)}, u32[]{:S(2)}) collective-permute-start(bf16[1024,128]{1,0:T(8,128)(2,1)S(1)} %get-tuple-element.63), channel_id=1, source_target_pairs={{0,4},{1,5},{2,6},{3,7},{4,0},{5,1},{6,2},{7,3},{8,12},{9,13},{10,... | collective-permute-start | bytes 786440 | tf_op jit(solution)/shard_map/ppermute | solution.py:406
  158.9 2.3 collective-permute-start.5
  161.3 3.5 %collective-permute-done.1 = bf16[1024,128]{1,0:T(8,128)(2,1)S(1)} collective-permute-done((bf16[1024,128]{1,0:T(8,128)(2,1)S(1)}, bf16[1024,128]{1,0:T(8,128)(2,1)S(1)}, u32[]{:S(2)}, u32[]{:S(2)}) %collective-permute-start.1) | collective-permute-done | bytes 262176 | tf_op jit(solution)/shard_map/ppermute | solution.py:406
  164.8 15.9 %collective-permute-done.2 = bf16[1024,128]{1,0:T(8,128)(2,1)S(1)} collective-permute-done((bf16[1024,128]{1,0:T(8,128)(2,1)S(1)}, bf16[1024,128]{1,0:T(8,128)(2,1)S(1)}, u32[]{:S(2)}, u32[]{:S(2)}) %collective-permute-start.2) | collective-permute-done | bytes 262176 | tf_op jit(solution)/shard_map/ppermute | solution.py:406
  180.7 1.1 collective-permute-done.6
  181.8 0.7 copy-done.13
  182.5 6.5 %second1.1 = bf16[8192,128]{1,0:T(8,128)(2,1)} custom-call(s32[1]{0:T(128)} %bitcast.24.r_0_.iy_ref, bf16[16,64,128]{2,1,0:T(8,128)(2,1)S(1)} %bitcast.67, bf16[16,64,128]{2,1,0:T(8,128)(2,1)S(1)} %bitcast.68, bf16[16,64,128]{2,1,0:T(8,128)(2,1)S(1)} %bitcast.69, bf16[16,64,128]{2,1,0:T(8,128)(2,1)S(1)} %bitcast.70, bf16[16,64,128]{2,1,0:T(8,128)(2,1)S(1)} %bitcast.71, ...), custom_call_target="tpu_custom_call" | custom-call | tf_op jit(solution)/shard_map/second1/pallas_call | solution.py:424
  189.0 7.1 %all-to-all-start.5 = ((bf16[16,512,128]{2,1,0:T(8,128)(2,1)}), bf16[16,512,128]{2,1,0:T(8,128)(2,1)S(1)}, u32[]{:S(2)}, u32[]{:S(2)}) async-start(bf16[16,512,128]{2,1,0:T(8,128)(2,1)} %bitcast.82), calls=%async_computation.5 | async-start | bytes 4194304 | tf_op jit(solution)/shard_map/all_to_all | solution.py:366
  196.1 0.6 reduce_sum.32
  197.3 11.7 %reshape.193 = f32[32,64,2,512]{3,2,1,0:T(2,128)} reshape(f32[2048,1024]{1,0:T(8,128)} %get-tuple-element.67) | data formatting | bytes 16777216 | tf_op jit(solution)/shard_map/reshape | solution.py:464
  209.0 4.2 %turn0.1.refs_0_ = bf16[32,128,256]{2,1,0:T(8,128)(2,1)} custom-call(bf16[16,32,16,128]{3,2,1,0:T(8,128)(2,1)} %bitcast.27.in_ref), custom_call_target="tpu_custom_call" | custom-call | tf_op jit(solution)/shard_map/turn0/pallas_call | solution.py:444
  213.2 17.1 %all-to-all-done.5 = bf16[16,512,128]{2,1,0:T(8,128)(2,1)S(1)} async-done(((bf16[16,512,128]{2,1,0:T(8,128)(2,1)}), bf16[16,512,128]{2,1,0:T(8,128)(2,1)S(1)}, u32[]{:S(2)}, u32[]{:S(2)}) %all-to-all-start.5) | async-done | bytes 2097184 | tf_op jit(solution)/shard_map/all_to_all | solution.py:366
  230.3 1.3 copy-done.11
  231.6 7.6 %first.1 = bf16[32,2,64,512]{3,2,1,0:T(8,128)(2,1)} custom-call(bf16[32,128,256]{2,1,0:T(8,128)(2,1)} %turn0.1.refs_0_, bf16[16,32,16,128]{3,2,1,0:T(8,128)(2,1)} %bitcast.83, bf16[1024,512]{1,0:T(8,128)(2,1)S(1)} %copy-done.2), custom_call_target="tpu_custom_call" | custom-call | tf_op jit(solution)/shard_map/first/pallas_call | solution.py:455
  (40 shorter events, 0.2 us)
Async XLA Ops:
  0.6 0.7 copy-start.5
  1.3 0.7 copy-start.6
  3.4 0.8 copy-start.3
  4.2 20.4 %all-to-all-start = ((s32[128,1,128]{2,1,0:T(1,128)}), s32[128,1,128]{2,1,0:T(1,128)S(1)}, u32[]{:S(2)}, u32[]{:S(2)}) async-start(s32[128,1,128]{2,1,0:T(1,128)} %bitcast.5), calls=%async_computation | async-start | bytes 131072 | tf_op jit(solution)/shard_map/all_to_all | solution.py:278
  33.8 7.8 %copy-start.17 = (f32[16]{0:T(128)S(1)}, f32[16]{0:T(128)}, u32[]{:S(2)}) copy-start(f32[16]{0:T(128)} %param.20) | copy-start | bytes 196
  33.8 9.1 %copy-start.14 = (f32[1,512,2]{1,2,0:T(2,128)S(1)}, f32[1,512,2]{1,2,0:T(2,128)}, u32[]{:S(2)}) copy-start(f32[1,512,2]{1,2,0:T(2,128)} %param.14) | copy-start | bytes 12292
  33.8 9.9 %copy-start.15 = (f32[64,2]{0,1:T(2,128)S(1)}, f32[64,2]{0,1:T(2,128)}, u32[]{:S(2)}) copy-start(f32[64,2]{0,1:T(2,128)} %param.19) | copy-start | bytes 1540
  33.8 11.8 %copy-start.12 = (bf16[1,512,2,128]{3,2,1,0:T(2,128)(2,1)S(1)}, bf16[1,512,2,128]{3,2,1,0:T(2,128)(2,1)}, u32[]{:S(2)}) copy-start(bf16[1,512,2,128]{3,2,1,0:T(2,128)(2,1)} %param.13) | copy-start | bytes 786436
  33.9 29.7 %all-to-all-start.1 = ((bf16[128,40,128]{2,1,0:T(8,128)(2,1)}), bf16[128,40,128]{2,1,0:T(8,128)(2,1)S(1)}, u32[]{:S(2)}, u32[]{:S(2)}) async-start(bf16[128,40,128]{2,1,0:T(8,128)(2,1)} %bitcast.10), calls=%async_computation.1 | async-start | bytes 2621440 | tf_op jit(solution)/shard_map/all_to_all | solution.py:300
  71.9 26.6 %all-to-all-start.2 = ((bf16[128,40,128]{2,1,0:T(8,128)(2,1)}), bf16[128,40,128]{2,1,0:T(8,128)(2,1)S(1)}, u32[]{:S(2)}, u32[]{:S(2)}) async-start(bf16[128,40,128]{2,1,0:T(8,128)(2,1)} %bitcast.85), calls=%async_computation.2 | async-start | bytes 2621440 | tf_op jit(solution)/shard_map/all_to_all | solution.py:346
  82.5 30.5 %copy-start.1 = (s32[2560,128]{1,0:T(8,128)}, s32[2560,128]{1,0:T(8,128)S(1)}, u32[]{:S(2)}) copy-start(s32[2560,128]{1,0:T(8,128)S(1)} %parts.1.part_ref.r_3_) | copy-start | bytes 3932164
  98.4 14.6 %copy-start = (bf16[128,40,128]{2,1,0:T(8,128)(2,1)}, bf16[128,40,128]{2,1,0:T(8,128)(2,1)S(1)}, u32[]{:S(2)}) copy-start(bf16[128,40,128]{2,1,0:T(8,128)(2,1)S(1)} %all-to-all-done.2) | copy-start | bytes 3932164
  113.0 3.6 %copy-start.4 = (s32[1,2560]{1,0:T(1,128)S(1)}, s32[1,2560]{1,0:T(1,128)}, u32[]{:S(2)}) copy-start(s32[1,2560]{1,0:T(1,128)} %shift_right_arithmetic.19.line_ref.r_2_) | copy-start | bytes 30724
  113.0 30.7 %all-to-all-start.3 = ((bf16[8,1024,128]{2,1,0:T(8,128)(2,1)}), bf16[8,1024,128]{2,1,0:T(8,128)(2,1)S(1)}, u32[]{:S(2)}, u32[]{:S(2)}) async-start(bf16[8,1024,128]{2,1,0:T(8,128)(2,1)} %get-tuple-element.48), calls=%async_computation.3 | async-start | bytes 4194304 | tf_op jit(solution)/shard_map/all_to_all | solution.py:389
  131.8 0.7 copy-start.7
  132.5 0.7 copy-start.9
  149.7 4.6 %copy-start.10 = (bf16[1024,128]{1,0:T(8,128)(2,1)S(1)}, bf16[1024,128]{1,0:T(8,128)(2,1)}, u32[]{:S(2)}) copy-start(bf16[1024,128]{1,0:T(8,128)(2,1)} %copy-done.9) | copy-start | bytes 786436
  149.7 4.7 %copy-start.8 = (bf16[1024,128]{1,0:T(8,128)(2,1)S(1)}, bf16[1024,128]{1,0:T(8,128)(2,1)}, u32[]{:S(2)}) copy-start(bf16[1024,128]{1,0:T(8,128)(2,1)} %copy-done.7) | copy-start | bytes 786436
  149.7 15.1 %copy-start.16 = (bf16[1024,128]{1,0:T(8,128)(2,1)S(1)}, bf16[1024,128]{1,0:T(8,128)(2,1)}, u32[]{:S(2)}) copy-start(bf16[1024,128]{1,0:T(8,128)(2,1)} %get-tuple-element.66) | copy-start | bytes 786436
  149.7 39.3 %all-to-all-start.4 = ((bf16[16,512,128]{2,1,0:T(8,128)(2,1)}), bf16[16,512,128]{2,1,0:T(8,128)(2,1)}, u32[]{:S(2)}, u32[]{:S(2)}) async-start(bf16[16,512,128]{2,1,0:T(8,128)(2,1)} %bitcast.81), calls=%async_computation.4 | async-start | bytes 4194304 | tf_op jit(solution)/shard_map/all_to_all | solution.py:366
  154.3 4.7 %collective-permute-start = (bf16[1024,128]{1,0:T(8,128)(2,1)S(1)}, bf16[1024,128]{1,0:T(8,128)(2,1)S(1)}, u32[]{:S(2)}, u32[]{:S(2)}) collective-permute-start(bf16[1024,128]{1,0:T(8,128)(2,1)S(1)} %copy-done.10), channel_id=1, source_target_pairs={{0,1},{1,0},{2,3},{3,2},{4,5},{5,4},{6,7},{7,6},{8,9},{9,8},{10,11... | collective-permute-start | bytes 786440 | tf_op jit(solution)/shard_map/ppermute | solution.py:406
  154.4 10.4 %collective-permute-start.1 = (bf16[1024,128]{1,0:T(8,128)(2,1)S(1)}, bf16[1024,128]{1,0:T(8,128)(2,1)S(1)}, u32[]{:S(2)}, u32[]{:S(2)}) collective-permute-start(bf16[1024,128]{1,0:T(8,128)(2,1)S(1)} %copy-done.8), channel_id=1, source_target_pairs={{0,2},{1,3},{2,4},{3,5},{4,6},{5,7},{6,0},{7,1},{8,10},{9,11},{10,... | collective-permute-start | bytes 786440 | tf_op jit(solution)/shard_map/ppermute | solution.py:406
  155.0 25.7 %collective-permute-start.2 = (bf16[1024,128]{1,0:T(8,128)(2,1)S(1)}, bf16[1024,128]{1,0:T(8,128)(2,1)S(1)}, u32[]{:S(2)}, u32[]{:S(2)}) collective-permute-start(bf16[1024,128]{1,0:T(8,128)(2,1)S(1)} %get-tuple-element.62), channel_id=1, source_target_pairs={{0,3},{1,2},{2,5},{3,4},{4,7},{5,6},{6,1},{7,0},{8,11},{9,10},{10,... | collective-permute-start | bytes 786440 | tf_op jit(solution)/shard_map/ppermute | solution.py:406
  155.1 25.6 %collective-permute-start.3 = (bf16[1024,128]{1,0:T(8,128)(2,1)S(1)}, bf16[1024,128]{1,0:T(8,128)(2,1)S(1)}, u32[]{:S(2)}, u32[]{:S(2)}) collective-permute-start(bf16[1024,128]{1,0:T(8,128)(2,1)S(1)} %get-tuple-element.63), channel_id=1, source_target_pairs={{0,4},{1,5},{2,6},{3,7},{4,0},{5,1},{6,2},{7,3},{8,12},{9,13},{10,... | collective-permute-start | bytes 786440 | tf_op jit(solution)/shard_map/ppermute | solution.py:406
  158.9 21.8 %collective-permute-start.4 = (bf16[1024,128]{1,0:T(8,128)(2,1)S(1)}, bf16[1024,128]{1,0:T(8,128)(2,1)S(1)}, u32[]{:S(2)}, u32[]{:S(2)}) collective-permute-start(bf16[1024,128]{1,0:T(8,128)(2,1)S(1)} %get-tuple-element.64), channel_id=1, source_target_pairs={{0,5},{1,4},{2,7},{3,6},{4,1},{5,0},{6,3},{7,2},{8,13},{9,12},{10,... | collective-permute-start | bytes 786440 | tf_op jit(solution)/shard_map/ppermute | solution.py:406
  158.9 21.8 %collective-permute-start.5 = (bf16[1024,128]{1,0:T(8,128)(2,1)S(1)}, bf16[1024,128]{1,0:T(8,128)(2,1)S(1)}, u32[]{:S(2)}, u32[]{:S(2)}) collective-permute-start(bf16[1024,128]{1,0:T(8,128)(2,1)S(1)} %get-tuple-element.65), channel_id=1, source_target_pairs={{0,6},{1,7},{2,0},{3,1},{4,2},{5,3},{6,4},{7,5},{8,14},{9,15},{10,... | collective-permute-start | bytes 786440 | tf_op jit(solution)/shard_map/ppermute | solution.py:406
  164.8 17.0 %collective-permute-start.6 = (bf16[1024,128]{1,0:T(8,128)(2,1)S(1)}, bf16[1024,128]{1,0:T(8,128)(2,1)S(1)}, u32[]{:S(2)}, u32[]{:S(2)}) collective-permute-start(bf16[1024,128]{1,0:T(8,128)(2,1)S(1)} %copy-done.16), channel_id=1, source_target_pairs={{0,7},{1,6},{2,1},{3,0},{4,3},{5,2},{6,5},{7,4},{8,15},{9,14},{10,... | collective-permute-start | bytes 786440 | tf_op jit(solution)/shard_map/ppermute | solution.py:406
  181.8 0.7 copy-start.13
  189.0 41.3 %all-to-all-start.5 = ((bf16[16,512,128]{2,1,0:T(8,128)(2,1)}), bf16[16,512,128]{2,1,0:T(8,128)(2,1)S(1)}, u32[]{:S(2)}, u32[]{:S(2)}) async-start(bf16[16,512,128]{2,1,0:T(8,128)(2,1)} %bitcast.82), calls=%async_computation.5 | async-start | bytes 4194304 | tf_op jit(solution)/shard_map/all_to_all | solution.py:366
  209.0 22.6 %copy-start.2 = (bf16[1024,512]{1,0:T(8,128)(2,1)S(1)}, bf16[1024,512]{1,0:T(8,128)(2,1)}, u32[]{:S(2)}) copy-start(bf16[1024,512]{1,0:T(8,128)(2,1)} %constant.65.clone.refs_2_) | copy-start | bytes 3145732
  230.3 1.3 copy-start.11
where the time goes:
time: 242 us; the launch traced here: 240 us
  waiting for transfers between devices  79.2 us (33%)
  Pallas kernels  73.3 us (30%)
  starting transfers between devices  45.9 us (19%)
  local copies, waits for them, and re-layouts  24.7 us (10%)
  other arithmetic  12.6 us (5%)
  between operations  4.59 us (2%)
    ppermute x7, waiting for transfers between devices, local(): arrived.append(lax.ppermute(pieces[k], 'gy', pairs))  20.5 us
    all_to_all x2, waiting for transfers between devices, cross(): lax.all_to_all(x, 'gx', split_axis=0, concat_axis=0, tiled=True)  17.1 us
    all_to_all x1, waiting for transfers between devices, local(): lax.all_to_all(outgoing.reshape(peers, 2 * CAP, block_len), ('gx', 'gy'),...  15.9 us
    pallas_call x1, Pallas kernels, local(): pl.pallas_call(lambda *r, first_line=start * local_b: insert_next(first_l...  15.2 us
    pallas_call x1, Pallas kernels, local(): pl.pallas_call(insert_first, grid=(steps,), out_shape=(update_shape, jax....  14.6 us
    all_to_all x1, waiting for transfers between devices, local(): lax.all_to_all(looked.reshape(peers, 2 * CAP, block_len), ('gx', 'gy'), s...  13.2 us
    reshape x1, local copies, waits for them, and re-layouts, local(): update = update.reshape(local_a, local_b, 2, length)  11.7 us
    all_to_all x2, starting transfers between devices, cross(): lax.all_to_all(x, 'gx', split_axis=0, concat_axis=0, tiled=True)  11.6 us
  transfers between devices with their start and end apart: 13, of which 8 were waited for; matrix products, arithmetic and copies ran while one was open for 13% of the time, Pallas kernels for 11%

commit v1 on v0

--- a/solution.py
+++ b/solution.py
@@ -72,7 +72,7 @@
     return ((iy // 2 + chips + direction * (k // 2)) % chips) * 2 + (iy % 2 + k % 2) % 2
 
 
-def slots_kernel(own_ref, bid_ref, sent_ref, row_ref, col_ref):
+def slots_kernel(own_ref, bid_ref, sent_ref, row_ref):
     peers = sent_ref.shape[0]
     own = jnp.concatenate([own_ref[0:1, :], own_ref[1:2, :]], axis=1)
     bid = jnp.concatenate([bid_ref[0:1, :], bid_ref[1:2, :]], axis=1)
@@ -91,10 +91,7 @@
     high_at = lax.dot_general(hot_b, high, nt, preferred_element_type=F32)
     low_at = lax.dot_general(hot_b, low, nt, preferred_element_type=F32)
     sent_ref[...] = (high_at * 64.0 + low_at - 64.0).astype(I32)
-    target = own * CAP + slot_i
-    row_ref[...] = target
-    wide = jnp.broadcast_to(target.astype(F32), (peers, count))
-    col_ref[...] = wide.T.astype(I32)
+    row_ref[...] = own * CAP + slot_i
 
 
 def lookup_kernel(ids_ref, vol_ref, out_ref, tmp_ref):
@@ -109,28 +106,29 @@
     out_ref[...] = tmp_ref[...].astype(BF)
 
 
-def parts_kernel(part_ref, out_ref):
-    wide = jnp.broadcast_to(part_ref[...].astype(F32), (out_ref.shape[1], out_ref.shape[0]))
-    out_ref[...] = wide.T.astype(I32)
-
-
 def split_parts(rows_ref, tmp_ref):
     tmp_ref[...] = rows_ref[...].astype(F32)
     count = tmp_ref.shape[0] // 2
     return tmp_ref[pl.ds(0, count, stride=2), :], tmp_ref[pl.ds(1, count, stride=2), :]
 
 
-def particle_kernel(ret_ref, col_ref, row_ref, w_ref, shift_ref, ctf_ref, out_ref, mis_ref, tmp_ref):
+def particle_kernel(
+    target_ref, ret_ref, row_ref, w_ref, shift_ref, ctf_ref, out_ref, mis_ref, tmp_ref, got_ref
+):
     total = ret_ref.shape[0] // 2
     tiles = w_ref.shape[0]
-    lanes = iota((2 * tiles, 128), 1)
-    col = col_ref[...]
-    real, imag = split_parts(ret_ref, tmp_ref)
-    blocks = jnp.concatenate([real, imag], axis=1).astype(BF)
-    pick = jnp.concatenate(
-        [jnp.where(col == lanes + 128 * b, 1.0, 0.0).astype(BF) for b in range(total // 128)], axis=1
-    )
-    fetched = dot(pick, blocks)
+    unroll = 16
+    tmp_ref[...] = ret_ref[...].astype(F32)
+
+    def fetch(i, carry):
+        at = pl.multiple_of(i * (2 * unroll), 8)
+        for u in range(unroll):
+            source = pl.multiple_of(2 * target_ref[0, i * unroll + u], 2)
+            got_ref[pl.ds(at + 2 * u, 2), :] = tmp_ref[pl.ds(source, 2), :]
+        return carry
+
+    lax.fori_loop(0, 2 * tiles // unroll, fetch, 0)
+    fetched = jnp.concatenate([got_ref[pl.ds(r, 2 * tiles, stride=2), :] for r in range(2)], axis=1)
     w0 = w_ref[:, 0:1]
     w1 = w_ref[:, 1:2]
     projected = w0 * fetched[:tiles] + w1 * fetched[tiles:]
@@ -151,35 +149,38 @@
     out_ref[...] = tmp_ref[...].astype(BF)
 
 
-def insert_lines(first_line, inc_ref, line_ref, part_ref, vol_ref, table_ref, upd_ref, tmp_ref, exp_ref):
-    total = exp_ref.shape[0]
-    lines = vol_ref.shape[0]
+def insert_lines(first_line, inc_ref, id_ref, vol_ref, table_ref, upd_ref, tmp_ref, block_ref):
+    total = block_ref.shape[0]
+    lines, width = vol_ref.shape
+    per_line = width // 256
 
     @pl.when(pl.program_id(0) == 0)
     def _():
-        part = part_ref[...]
         for r, inc in enumerate(split_parts(inc_ref, tmp_ref)):
-            for m in range(4):
-                exp_ref[:, (r * 4 + m) * 128 : (r * 4 + m + 1) * 128] = jnp.where(part == m, inc, 0.0).astype(BF)
+            block_ref[:, r * 128 : (r + 1) * 128] = inc.astype(BF)
 
     base = first_line + pl.program_id(0) * lines
-    pick = jnp.where(iota((lines, total), 0) + base == line_ref[...], 1.0, 0.0).astype(BF)
-    update = dot(pick, exp_ref[...])
+    block_id = (iota((lines, total), 0) + base) * per_line
+    sums = []
+    for m in range(per_line):
+        pick = jnp.where(block_id + m == id_ref[...], 1.0, 0.0).astype(BF)
+        sums.append(dot(pick, block_ref[...]))
+    update = jnp.concatenate([x[:, r * 128 : (r + 1) * 128] for r in range(2) for x in sums], axis=1)
     upd_ref[...] = update
     inserted = (vol_ref[...].astype(F32) + update).astype(BF)
     return dot(inserted, table_ref[...])
 
 
-def insert_first(inc_ref, line_ref, part_ref, vol_ref, table_ref, upd_ref, out_ref, tmp_ref, exp_ref):
-    passed = insert_lines(0, inc_ref, line_ref, part_ref, vol_ref, table_ref, upd_ref, tmp_ref, exp_ref)
+def insert_first(inc_ref, id_ref, vol_ref, table_ref, upd_ref, out_ref, tmp_ref, block_ref):
+    passed = insert_lines(0, inc_ref, id_ref, vol_ref, table_ref, upd_ref, tmp_ref, block_ref)
     for d in range(out_ref.shape[0]):
         out_ref[d] = passed[:, d * 128 : (d + 1) * 128].astype(BF)
 
 
-def insert_next(first_line, iy_ref, inc_ref, line_ref, part_ref, vol_ref, table_ref, old_ref, upd_ref, *refs):
+def insert_next(first_line, iy_ref, inc_ref, id_ref, vol_ref, table_ref, old_ref, upd_ref, *refs):
     outs = refs[:-3]
-    tmp_ref, exp_ref, pass_ref = refs[-3:]
-    passed = insert_lines(first_line, inc_ref, line_ref, part_ref, vol_ref, table_ref, upd_ref, tmp_ref, exp_ref)
+    tmp_ref, block_ref, pass_ref = refs[-3:]
+    passed = insert_lines(first_line, inc_ref, id_ref, vol_ref, table_ref, upd_ref, tmp_ref, block_ref)
     pass_ref[...] = passed.astype(BF)
     for k, out_ref in enumerate(outs):
         dest = shifted_index(iy_ref[0], k, len(outs), 1)
@@ -263,15 +264,14 @@
 
     own = owners.transpose(0, 2, 1).reshape(2, tiles)
     bid = block_ids.transpose(0, 2, 1).reshape(2, tiles)
-    sent, row, col = pl.pallas_call(
+    sent, row = pl.pallas_call(
         slots_kernel,
         out_shape=(
             jax.ShapeDtypeStruct((peers, 128), I32),
             jax.ShapeDtypeStruct((1, refs), I32),
-            jax.ShapeDtypeStruct((refs, 128), I32),
         ),
         in_specs=[whole] * 2,
-        out_specs=(whole,) * 3,
+        out_specs=(whole,) * 2,
         compiler_params=params(),
         name="slots",
     )(own, bid)
@@ -314,22 +314,9 @@
     shifted = jnp.concatenate([spec_re * cosine - spec_im * sine, spec_re * sine + spec_im * cosine], axis=1)
     ctf = -jnp.sin(defocus_part[0] * radius_sq + 0.1)
 
-    ids = jnp.maximum(got[:, :CAP].reshape(1, total), -4)
-    line_row = ids >> 2
-    part_row = ids & 3
+    ids = got[:, :CAP].reshape(1, total)
     weight = weights.reshape(tiles, 2)
-    returned, line_row, part_row, weight, shifted, ctf = lax.optimization_barrier(
-        (returned, line_row, part_row, weight, shifted, ctf)
-    )
-    part_col = pl.pallas_call(
-        parts_kernel,
-        out_shape=jax.ShapeDtypeStruct((total, 128), I32),
-        in_specs=[whole],
-        out_specs=whole,
-        compiler_params=params(),
-        cost_estimate=pl.CostEstimate(flops=1 << 22, bytes_accessed=1 << 22, transcendentals=0),
-        name="parts",
-    )(part_row)
+    returned, ids, weight, shifted, ctf = lax.optimization_barrier((returned, ids, weight, shifted, ctf))
 
     outgoing, squares = pl.pallas_call(
         particle_kernel,
@@ -337,21 +324,20 @@
             jax.ShapeDtypeStruct((rows, block_len), BF),
             jax.ShapeDtypeStruct((1, 2 * block_len), F32),
         ),
-        in_specs=[whole] * 6,
+        in_specs=[scalars] + [whole] * 5,
         out_specs=(whole,) * 2,
-        scratch_shapes=[pltpu.VMEM((rows, block_len), F32)],
+        scratch_shapes=[pltpu.VMEM((rows, block_len), F32), pltpu.VMEM((2 * refs, block_len), F32)],
         compiler_params=params(),
         name="particle",
-    )(near(returned), col, row, weight, shifted, ctf)
+    )(row, near(returned), row, weight, shifted, ctf)
     incoming = lax.all_to_all(
         outgoing.reshape(peers, 2 * CAP, block_len), ("gx", "gy"), split_axis=0, concat_axis=0, tiled=True
     ).reshape(rows, block_len)
     misfit = (jnp.sum(squares) / (2.0 * tiles * block_len)).reshape(1)
-    incoming, part_col = lax.optimization_barrier((incoming, part_col))
 
     iy = lax.axis_index("gy").astype(I32).reshape(1)
     step = 256
-    insert_scratch = [pltpu.VMEM((rows, block_len), F32), pltpu.VMEM((total, 2 * length), BF)]
+    insert_scratch = [pltpu.VMEM((rows, block_len), F32), pltpu.VMEM((total, 2 * block_len), BF)]
     update_shape = jax.ShapeDtypeStruct((lines, 2 * length), F32)
 
     def second_shapes(count):
@@ -380,25 +366,25 @@
                 insert_first,
                 grid=(steps,),
                 out_shape=(update_shape, jax.ShapeDtypeStruct((gy, chunk_lines, 128), BF)),
-                in_specs=[whole] * 3 + [block, whole],
+                in_specs=[whole] * 2 + [block, whole],
                 out_specs=(block, pl.BlockSpec((gy, step, 128), lambda i: (0, i, 0))),
                 scratch_shapes=insert_scratch,
                 compiler_params=params(dimension_semantics=("arbitrary",)),
                 name="insert0",
-            )(near(incoming), line_row, near(part_col), vol, third)
+            )(near(incoming), ids, vol, third)
             arrived = lax.all_to_all(out, "gy", split_axis=0, concat_axis=0, tiled=True)
         else:
             update, *pieces = pl.pallas_call(
                 lambda *r, first_line=start * local_b: insert_next(first_line, *r),
                 grid=(steps,),
                 out_shape=(update_shape,) + (jax.ShapeDtypeStruct((chunk_lines, 128), BF),) * gy,
-                in_specs=[scalars] + [whole] * 3 + [block, whole, pl.BlockSpec(memory_space=pl.ANY)],
+                in_specs=[scalars] + [whole] * 2 + [block, whole, pl.BlockSpec(memory_space=pl.ANY)],
                 out_specs=(block,) + (pl.BlockSpec((step, 128), lambda i: (i, 0)),) * gy,
                 scratch_shapes=insert_scratch + [pltpu.VMEM((step, 2 * length), BF)],
-                input_output_aliases={6: 0},
+                input_output_aliases={5: 0},
                 compiler_params=params(dimension_semantics=("arbitrary",)),
                 name=f"insert{j}",
-            )(iy, incoming, line_row, part_col, vol, third, update)
+            )(iy, incoming, ids, vol, third, update)
             before, pieces = lax.optimization_barrier((before, pieces))
             arrived = [pieces[0]]
             for k in range(1, gy):

time: 242 us -> 234 us (0.967)
  Pallas kernels: 73.3 us -> 64.3 us
  waiting for transfers between devices: 79.2 us -> 83.2 us
  local copies, waits for them, and re-layouts: 24.7 us -> 21.8 us
    pallas_call x1, Pallas kernels: 15.2 us -> 12.2 us  [local(): pl.pallas_call(lambda *r, first_line=start * local_b: insert_next(first_l...]
    all_to_all x1, waiting for transfers between devices: 10.5 us -> 13.4 us  [local(): arrived = lax.all_to_all(out, 'gy', split_axis=0, concat_axis=0, tiled=True)]
    pallas_call x1, Pallas kernels: 14.6 us -> 11.7 us  [local(): pl.pallas_call(insert_first, grid=(steps,), out_shape=(update_shape, jax....]
    pallas_call x1, Pallas kernels: 8.3 us -> 5.61 us  [local(): pl.pallas_call(particle_kernel, out_shape=(jax.ShapeDtypeStruct((rows, bl...]
    unnamed x38 -> x30, local copies, waits for them, and re-layouts: 11.2 us -> 9.03 us
  transfers between devices with their start and end apart: 13 -> 13, of which waited for: 8 -> 8; matrix products, arithmetic and copies ran while one was open for 13% -> 13% of each run, Pallas kernels for 11% -> 10%
where the time goes in v1:
time: 234 us; the launch traced here: 232 us
  waiting for transfers between devices  83.2 us (36%)
  Pallas kernels  64.3 us (27%)
  starting transfers between devices  45.4 us (19%)
  local copies, waits for them, and re-layouts  21.8 us (9%)
  other arithmetic  12.7 us (5%)
  between operations  4.59 us (2%)
    ppermute x7, waiting for transfers between devices, local(): arrived.append(lax.ppermute(pieces[k], 'gy', pairs))  20.5 us
    all_to_all x2, waiting for transfers between devices, cross(): lax.all_to_all(x, 'gx', split_axis=0, concat_axis=0, tiled=True)  17 us
    all_to_all x1, waiting for transfers between devices, local(): lax.all_to_all(outgoing.reshape(peers, 2 * CAP, block_len), ('gx', 'gy'),...  16.5 us
    all_to_all x1, waiting for transfers between devices, local(): arrived = lax.all_to_all(out, 'gy', split_axis=0, concat_axis=0, tiled=True)  13.4 us
    all_to_all x1, waiting for transfers between devices, local(): lax.all_to_all(looked.reshape(peers, 2 * CAP, block_len), ('gx', 'gy'), s...  13.2 us
    pallas_call x1, Pallas kernels, local(): pl.pallas_call(lambda *r, first_line=start * local_b: insert_next(first_l...  12.2 us
    pallas_call x1, Pallas kernels, local(): pl.pallas_call(insert_first, grid=(steps,), out_shape=(update_shape, jax....  11.7 us
    all_to_all x2, starting transfers between devices, cross(): lax.all_to_all(x, 'gx', split_axis=0, concat_axis=0, tiled=True)  11.7 us
  transfers between devices with their start and end apart: 13, of which 8 were waited for; matrix products, arithmetic and copies ran while one was open for 13% of the time, Pallas kernels for 10%

profile of v1, /device:TPU:0, one launch (start us, length us, event | category | flops | bytes accessed | tf_op | source)
XLA Modules:
  0.0 232.0 jit_solution(3326477952801962879)
XLA Ops:
  0.6 0.7 copy-done.2
  1.3 0.7 copy-done.3
  2.0 1.3 slots.1
  3.3 11.2 %all-to-all-start = ((s32[128,1,128]{2,1,0:T(1,128)}), s32[128,1,128]{2,1,0:T(1,128)S(1)}, u32[]{:S(2)}, u32[]{:S(2)}) async-start(s32[128,1,128]{2,1,0:T(1,128)} %bitcast.5), calls=%async_computation | async-start | bytes 131072 | tf_op jit(solution)/shard_map/all_to_all | solution.py:278
  14.5 6.6 %convert.7 = f32[2048,2,4,128]{3,1,2,0:T(2,128)} convert(bf16[2048,2,4,128]{3,1,2,0:T(2,128)(2,1)} %bitcast.80) | non-fusion elementwise | flops 2097152 | bytes 12582912 | tf_op jit(solution)/shard_map/reshape | solution.py:289
  21.1 2.6 %all-to-all-done = s32[128,1,128]{2,1,0:T(1,128)S(1)} async-done(((s32[128,1,128]{2,1,0:T(1,128)}), s32[128,1,128]{2,1,0:T(1,128)S(1)}, u32[]{:S(2)}, u32[]{:S(2)}) %all-to-all-start) | async-done | bytes 65568 | tf_op jit(solution)/shard_map/all_to_all | solution.py:278
  23.7 9.3 %lookup.1 = bf16[5120,128]{1,0:T(8,128)(2,1)} custom-call(s32[128,128]{1,0:T(8,128)S(1)} %bitcast.66, f32[16384,128]{1,0:T(8,128)} %bitcast.79), custom_call_target="tpu_custom_call" | custom-call | tf_op jit(solution)/shard_map/lookup/pallas_call | solution.py:291
  33.0 7.1 %all-to-all-start.1 = ((bf16[128,40,128]{2,1,0:T(8,128)(2,1)}), bf16[128,40,128]{2,1,0:T(8,128)(2,1)S(1)}, u32[]{:S(2)}, u32[]{:S(2)}) async-start(bf16[128,40,128]{2,1,0:T(8,128)(2,1)} %bitcast.10), calls=%async_computation.1 | async-start | bytes 2621440 | tf_op jit(solution)/shard_map/all_to_all | solution.py:300
  41.5 0.1 copy.26
  41.7 0.7 fusion.9
  43.1 0.1 select_reduce_fusion
  43.2 0.6 fusion.11
  43.8 1.2 sine_negate_fusion.ctf_ref
  45.0 0.4 fusion.10
  45.4 2.6 %fusion = (f32[512,128]{1,0:T(8,128)S(1)}, f32[512,128]{1,0:T(8,128)S(1)}) fusion(f32[]{:T(128)} %bitcast.17, f32[]{:T(128)} %bitcast.16, bf16[1,512,1,128]{3,2,1,0:T(2,128)(2,1)S(1)} %get-tuple-element.64, bf16[1,512,1,128]{3,2,1,0:T(2,128)(2,1)S(1)} %get-tuple-element.63), kind=kLoop, calls=%fused_computation.12 | loop fusion | flops 2686976 | bytes 786440 | tf_op jit(solution)/shard_map/sub | solution.py:314
  48.0 0.8 pad_maximum_fusion.shift_ref
  48.8 0.1 reshape.144.id_ref.r_2_
  48.9 13.2 %all-to-all-done.1 = bf16[128,40,128]{2,1,0:T(8,128)(2,1)S(1)} async-done(((bf16[128,40,128]{2,1,0:T(8,128)(2,1)}), bf16[128,40,128]{2,1,0:T(8,128)(2,1)S(1)}, u32[]{:S(2)}, u32[]{:S(2)}) %all-to-all-start.1) | async-done | bytes 1310752 | tf_op jit(solution)/shard_map/all_to_all | solution.py:300
  62.1 5.6 %particle.1 = (bf16[5120,128]{1,0:T(8,128)(2,1)}, f32[1,256]{1,0:T(1,128)S(1)}) custom-call(s32[1,1024]{1,0:T(1,128)S(1)} %get-tuple-element.32.target_ref.row_ref, bf16[5120,128]{1,0:T(8,128)(2,1)S(1)} %bitcast.64, s32[1,1024]{1,0:T(1,128)S(1)} %get-tuple-element.32.target_ref.row_ref, f32[512,2]{1,0:T(8,128)S(1)} %bitcast.65, ...), custom_call_target="tpu_custom_call" | custom-call | tf_op jit(solution)/shard_map/particle/pallas_call | solution.py:321
  67.7 4.6 %all-to-all-start.2 = ((bf16[128,40,128]{2,1,0:T(8,128)(2,1)}), bf16[128,40,128]{2,1,0:T(8,128)(2,1)S(1)}, u32[]{:S(2)}, u32[]{:S(2)}) async-start(bf16[128,40,128]{2,1,0:T(8,128)(2,1)} %bitcast.85), calls=%async_computation.2 | async-start | bytes 2621440 | tf_op jit(solution)/shard_map/all_to_all | solution.py:333
  72.4 5.4 %copy.31 = bf16[256,8,2,512]{3,1,2,0:T(8,128)(2,1)} copy(bf16[256,8,2,512]{3,2,1,0:T(2,128)(2,1)} %bitcast.81) | data formatting | bytes 8388608
  77.8 16.5 %all-to-all-done.2 = bf16[128,40,128]{2,1,0:T(8,128)(2,1)S(1)} async-done(((bf16[128,40,128]{2,1,0:T(8,128)(2,1)}), bf16[128,40,128]{2,1,0:T(8,128)(2,1)S(1)}, u32[]{:S(2)}, u32[]{:S(2)}) %all-to-all-start.2) | async-done | bytes 1310752 | tf_op jit(solution)/shard_map/all_to_all | solution.py:333
  94.3 11.7 %insert0.1 = (f32[2048,1024]{1,0:T(8,128)}, bf16[8,1024,128]{2,1,0:T(8,128)(2,1)}) custom-call(bf16[5120,128]{1,0:T(8,128)(2,1)S(1)} %bitcast.61, s32[1,2560]{1,0:T(1,128)S(1)} %reshape.144.id_ref.r_2_, bf16[2048,1024]{1,0:T(8,128)(2,1)} %bitcast.77, bf16[1024,1024]{1,0:T(8,128)(2,1)} %constant.57.clone.table_ref.r_4_), custom_call_target="tpu_custom_call" | custom-call | tf_op jit(solution)/shard_map/insert0/pallas_call | solution.py:365
  106.0 3.8 %all-to-all-start.3 = ((bf16[8,1024,128]{2,1,0:T(8,128)(2,1)}), bf16[8,1024,128]{2,1,0:T(8,128)(2,1)S(1)}, u32[]{:S(2)}, u32[]{:S(2)}) async-start(bf16[8,1024,128]{2,1,0:T(8,128)(2,1)} %get-tuple-element.40), calls=%async_computation.3 | async-start | bytes 4194304 | tf_op jit(solution)/shard_map/all_to_all | solution.py:375
  109.8 12.2 %insert1.1 = (f32[2048,1024]{1,0:T(8,128)}, bf16[1024,128]{1,0:T(8,128)(2,1)S(1)}, bf16[1024,128]{1,0:T(8,128)(2,1)S(1)}, bf16[1024,128]{1,0:T(8,128)(2,1)S(1)},...) custom-call(s32[1]{0:T(128)} %bitcast.24.r_0_.iy_ref, ...), custom_call_target="tpu_custom_call", output_to_operand_aliasing={{0}: (5, {})} | custom-call | tf_op jit(solution)/shard_map/insert1/pallas_call | solution.py:377
  122.0 0.7 copy-done.4
  122.7 0.7 copy-done.6
  123.4 13.4 %all-to-all-done.3 = bf16[8,1024,128]{2,1,0:T(8,128)(2,1)S(1)} async-done(((bf16[8,1024,128]{2,1,0:T(8,128)(2,1)}), bf16[8,1024,128]{2,1,0:T(8,128)(2,1)S(1)}, u32[]{:S(2)}, u32[]{:S(2)}) %all-to-all-start.3) | async-done | bytes 2097184 | tf_op jit(solution)/shard_map/all_to_all | solution.py:375
  136.8 5.9 %second0.1 = bf16[8192,128]{1,0:T(8,128)(2,1)} custom-call(bf16[8,16,64,128]{3,2,1,0:T(8,128)(2,1)S(1)} %bitcast.63, bf16[512,1024]{1,0:T(8,128)(2,1)} %constant.58.clone.table_ref.refs_8_), custom_call_target="tpu_custom_call" | custom-call | tf_op jit(solution)/shard_map/second0/pallas_call | solution.py:402
  142.7 4.6 %all-to-all-start.4 = ((bf16[16,512,128]{2,1,0:T(8,128)(2,1)}), bf16[16,512,128]{2,1,0:T(8,128)(2,1)}, u32[]{:S(2)}, u32[]{:S(2)}) async-start(bf16[16,512,128]{2,1,0:T(8,128)(2,1)} %bitcast.82), calls=%async_computation.4 | async-start | bytes 4194304 | tf_op jit(solution)/shard_map/all_to_all | solution.py:352
  147.3 0.1 collective-permute-start
  147.4 0.6 collective-permute-start.1
  148.0 0.1 collective-permute-start.2
  148.1 3.8 %collective-permute-start.3 = (bf16[1024,128]{1,0:T(8,128)(2,1)S(1)}, bf16[1024,128]{1,0:T(8,128)(2,1)S(1)}, u32[]{:S(2)}, u32[]{:S(2)}) collective-permute-start(bf16[1024,128]{1,0:T(8,128)(2,1)S(1)} %get-tuple-element.55), channel_id=1, source_target_pairs={{0,4},{1,5},{2,6},{3,7},{4,0},{5,1},{6,2},{7,3},{8,12},{9,13},{10,... | collective-permute-start | bytes 786440 | tf_op jit(solution)/shard_map/ppermute | solution.py:392
  151.9 0.0 collective-permute-start.4
  151.9 2.3 collective-permute-start.5
  154.2 3.5 %collective-permute-done.1 = bf16[1024,128]{1,0:T(8,128)(2,1)S(1)} collective-permute-done((bf16[1024,128]{1,0:T(8,128)(2,1)S(1)}, bf16[1024,128]{1,0:T(8,128)(2,1)S(1)}, u32[]{:S(2)}, u32[]{:S(2)}) %collective-permute-start.1) | collective-permute-done | bytes 262176 | tf_op jit(solution)/shard_map/ppermute | solution.py:392
  157.7 0.0 collective-permute-start.6
  157.8 15.9 %collective-permute-done.2 = bf16[1024,128]{1,0:T(8,128)(2,1)S(1)} collective-permute-done((bf16[1024,128]{1,0:T(8,128)(2,1)S(1)}, bf16[1024,128]{1,0:T(8,128)(2,1)S(1)}, u32[]{:S(2)}, u32[]{:S(2)}) %collective-permute-start.2) | collective-permute-done | bytes 262176 | tf_op jit(solution)/shard_map/ppermute | solution.py:392
  173.7 1.1 collective-permute-done.6
  174.7 0.7 copy-done.9
  175.4 6.4 %second1.1 = bf16[8192,128]{1,0:T(8,128)(2,1)} custom-call(s32[1]{0:T(128)} %bitcast.24.r_0_.iy_ref, bf16[16,64,128]{2,1,0:T(8,128)(2,1)S(1)} %bitcast.68, bf16[16,64,128]{2,1,0:T(8,128)(2,1)S(1)} %bitcast.69, bf16[16,64,128]{2,1,0:T(8,128)(2,1)S(1)} %bitcast.70, bf16[16,64,128]{2,1,0:T(8,128)(2,1)S(1)} %bitcast.71, bf16[16,64,128]{2,1,0:T(8,128)(2,1)S(1)} %bitcast.72, ...), custom_call_target="tpu_custom_call" | custom-call | tf_op jit(solution)/shard_map/second1/pallas_call | solution.py:410
  181.9 7.2 %all-to-all-start.5 = ((bf16[16,512,128]{2,1,0:T(8,128)(2,1)}), bf16[16,512,128]{2,1,0:T(8,128)(2,1)}, u32[]{:S(2)}, u32[]{:S(2)}) async-start(bf16[16,512,128]{2,1,0:T(8,128)(2,1)} %bitcast.83), calls=%async_computation.5 | async-start | bytes 4194304 | tf_op jit(solution)/shard_map/all_to_all | solution.py:352
  189.0 0.6 reduce_sum.32
  190.3 11.7 %reshape.166 = f32[32,64,2,512]{3,2,1,0:T(2,128)} reshape(f32[2048,1024]{1,0:T(8,128)} %get-tuple-element.59) | data formatting | bytes 16777216 | tf_op jit(solution)/shard_map/reshape | solution.py:450
  202.0 4.2 %turn0.1.refs_0_ = bf16[32,128,256]{2,1,0:T(8,128)(2,1)} custom-call(bf16[16,32,16,128]{3,2,1,0:T(8,128)(2,1)} %bitcast.27.in_ref), custom_call_target="tpu_custom_call" | custom-call | tf_op jit(solution)/shard_map/turn0/pallas_call | solution.py:430
  206.2 17.0 %all-to-all-done.5 = bf16[16,512,128]{2,1,0:T(8,128)(2,1)} async-done(((bf16[16,512,128]{2,1,0:T(8,128)(2,1)}), bf16[16,512,128]{2,1,0:T(8,128)(2,1)}, u32[]{:S(2)}, u32[]{:S(2)}) %all-to-all-start.5) | async-done | bytes 2097184 | tf_op jit(solution)/shard_map/all_to_all | solution.py:352
  223.2 7.6 %first.1 = bf16[32,2,64,512]{3,2,1,0:T(8,128)(2,1)} custom-call(bf16[32,128,256]{2,1,0:T(8,128)(2,1)} %turn0.1.refs_0_, bf16[16,32,16,128]{3,2,1,0:T(8,128)(2,1)} %bitcast.37.refs_1_, bf16[1024,512]{1,0:T(8,128)(2,1)S(1)} %copy-done.1), custom_call_target="tpu_custom_call" | custom-call | tf_op jit(solution)/shard_map/first/pallas_call | solution.py:441
  (29 shorter events, 0.1 us)
Async XLA Ops:
  0.6 0.7 copy-start.2
  1.3 0.7 copy-start.3
  3.3 20.4 %all-to-all-start = ((s32[128,1,128]{2,1,0:T(1,128)}), s32[128,1,128]{2,1,0:T(1,128)S(1)}, u32[]{:S(2)}, u32[]{:S(2)}) async-start(s32[128,1,128]{2,1,0:T(1,128)} %bitcast.5), calls=%async_computation | async-start | bytes 131072 | tf_op jit(solution)/shard_map/all_to_all | solution.py:278
  33.0 8.5 %copy-start.10 = (f32[1,512,2]{1,2,0:T(2,128)S(1)}, f32[1,512,2]{1,2,0:T(2,128)}, u32[]{:S(2)}) copy-start(f32[1,512,2]{1,2,0:T(2,128)} %param.14) | copy-start | bytes 12292
  33.0 8.6 %copy-start.13 = (f32[16]{0:T(128)S(1)}, f32[16]{0:T(128)}, u32[]{:S(2)}) copy-start(f32[16]{0:T(128)} %param.20) | copy-start | bytes 196
  33.0 10.0 %copy-start.11 = (f32[64,2]{0,1:T(2,128)S(1)}, f32[64,2]{0,1:T(2,128)}, u32[]{:S(2)}) copy-start(f32[64,2]{0,1:T(2,128)} %param.19) | copy-start | bytes 1540
  33.0 11.9 %copy-start.8 = (bf16[1,512,2,128]{3,2,1,0:T(2,128)(2,1)S(1)}, bf16[1,512,2,128]{3,2,1,0:T(2,128)(2,1)}, u32[]{:S(2)}) copy-start(bf16[1,512,2,128]{3,2,1,0:T(2,128)(2,1)} %param.13) | copy-start | bytes 786436
  33.0 29.1 %all-to-all-start.1 = ((bf16[128,40,128]{2,1,0:T(8,128)(2,1)}), bf16[128,40,128]{2,1,0:T(8,128)(2,1)S(1)}, u32[]{:S(2)}, u32[]{:S(2)}) async-start(bf16[128,40,128]{2,1,0:T(8,128)(2,1)} %bitcast.10), calls=%async_computation.1 | async-start | bytes 2621440 | tf_op jit(solution)/shard_map/all_to_all | solution.py:300
  67.7 26.6 %all-to-all-start.2 = ((bf16[128,40,128]{2,1,0:T(8,128)(2,1)}), bf16[128,40,128]{2,1,0:T(8,128)(2,1)S(1)}, u32[]{:S(2)}, u32[]{:S(2)}) async-start(bf16[128,40,128]{2,1,0:T(8,128)(2,1)} %bitcast.85), calls=%async_computation.2 | async-start | bytes 2621440 | tf_op jit(solution)/shard_map/all_to_all | solution.py:333
  94.3 11.8 %copy-start = (bf16[128,40,128]{2,1,0:T(8,128)(2,1)}, bf16[128,40,128]{2,1,0:T(8,128)(2,1)S(1)}, u32[]{:S(2)}) copy-start(bf16[128,40,128]{2,1,0:T(8,128)(2,1)S(1)} %all-to-all-done.2) | copy-start | bytes 3932164
  106.0 30.7 %all-to-all-start.3 = ((bf16[8,1024,128]{2,1,0:T(8,128)(2,1)}), bf16[8,1024,128]{2,1,0:T(8,128)(2,1)S(1)}, u32[]{:S(2)}, u32[]{:S(2)}) async-start(bf16[8,1024,128]{2,1,0:T(8,128)(2,1)} %get-tuple-element.40), calls=%async_computation.3 | async-start | bytes 4194304 | tf_op jit(solution)/shard_map/all_to_all | solution.py:375
  122.0 0.7 copy-start.4
  122.7 0.7 copy-start.6
  142.7 4.6 %copy-start.7 = (bf16[1024,128]{1,0:T(8,128)(2,1)S(1)}, bf16[1024,128]{1,0:T(8,128)(2,1)}, u32[]{:S(2)}) copy-start(bf16[1024,128]{1,0:T(8,128)(2,1)} %copy-done.6) | copy-start | bytes 786436
  142.7 4.7 %copy-start.5 = (bf16[1024,128]{1,0:T(8,128)(2,1)S(1)}, bf16[1024,128]{1,0:T(8,128)(2,1)}, u32[]{:S(2)}) copy-start(bf16[1024,128]{1,0:T(8,128)(2,1)} %copy-done.4) | copy-start | bytes 786436
  142.7 15.1 %copy-start.12 = (bf16[1024,128]{1,0:T(8,128)(2,1)S(1)}, bf16[1024,128]{1,0:T(8,128)(2,1)}, u32[]{:S(2)}) copy-start(bf16[1024,128]{1,0:T(8,128)(2,1)} %get-tuple-element.58) | copy-start | bytes 786436
  142.7 39.2 %all-to-all-start.4 = ((bf16[16,512,128]{2,1,0:T(8,128)(2,1)}), bf16[16,512,128]{2,1,0:T(8,128)(2,1)}, u32[]{:S(2)}, u32[]{:S(2)}) async-start(bf16[16,512,128]{2,1,0:T(8,128)(2,1)} %bitcast.82), calls=%async_computation.4 | async-start | bytes 4194304 | tf_op jit(solution)/shard_map/all_to_all | solution.py:352
  147.3 4.7 %collective-permute-start = (bf16[1024,128]{1,0:T(8,128)(2,1)S(1)}, bf16[1024,128]{1,0:T(8,128)(2,1)S(1)}, u32[]{:S(2)}, u32[]{:S(2)}) collective-permute-start(bf16[1024,128]{1,0:T(8,128)(2,1)S(1)} %copy-done.7), channel_id=1, source_target_pairs={{0,1},{1,0},{2,3},{3,2},{4,5},{5,4},{6,7},{7,6},{8,9},{9,8},{10,11... | collective-permute-start | bytes 786440 | tf_op jit(solution)/shard_map/ppermute | solution.py:392
  147.4 10.4 %collective-permute-start.1 = (bf16[1024,128]{1,0:T(8,128)(2,1)S(1)}, bf16[1024,128]{1,0:T(8,128)(2,1)S(1)}, u32[]{:S(2)}, u32[]{:S(2)}) collective-permute-start(bf16[1024,128]{1,0:T(8,128)(2,1)S(1)} %copy-done.5), channel_id=1, source_target_pairs={{0,2},{1,3},{2,4},{3,5},{4,6},{5,7},{6,0},{7,1},{8,10},{9,11},{10,... | collective-permute-start | bytes 786440 | tf_op jit(solution)/shard_map/ppermute | solution.py:392
  148.0 25.7 %collective-permute-start.2 = (bf16[1024,128]{1,0:T(8,128)(2,1)S(1)}, bf16[1024,128]{1,0:T(8,128)(2,1)S(1)}, u32[]{:S(2)}, u32[]{:S(2)}) collective-permute-start(bf16[1024,128]{1,0:T(8,128)(2,1)S(1)} %get-tuple-element.54), channel_id=1, source_target_pairs={{0,3},{1,2},{2,5},{3,4},{4,7},{5,6},{6,1},{7,0},{8,11},{9,10},{10,... | collective-permute-start | bytes 786440 | tf_op jit(solution)/shard_map/ppermute | solution.py:392
  148.1 25.6 %collective-permute-start.3 = (bf16[1024,128]{1,0:T(8,128)(2,1)S(1)}, bf16[1024,128]{1,0:T(8,128)(2,1)S(1)}, u32[]{:S(2)}, u32[]{:S(2)}) collective-permute-start(bf16[1024,128]{1,0:T(8,128)(2,1)S(1)} %get-tuple-element.55), channel_id=1, source_target_pairs={{0,4},{1,5},{2,6},{3,7},{4,0},{5,1},{6,2},{7,3},{8,12},{9,13},{10,... | collective-permute-start | bytes 786440 | tf_op jit(solution)/shard_map/ppermute | solution.py:392
  151.9 21.8 %collective-permute-start.4 = (bf16[1024,128]{1,0:T(8,128)(2,1)S(1)}, bf16[1024,128]{1,0:T(8,128)(2,1)S(1)}, u32[]{:S(2)}, u32[]{:S(2)}) collective-permute-start(bf16[1024,128]{1,0:T(8,128)(2,1)S(1)} %get-tuple-element.56), channel_id=1, source_target_pairs={{0,5},{1,4},{2,7},{3,6},{4,1},{5,0},{6,3},{7,2},{8,13},{9,12},{10,... | collective-permute-start | bytes 786440 | tf_op jit(solution)/shard_map/ppermute | solution.py:392
  151.9 21.8 %collective-permute-start.5 = (bf16[1024,128]{1,0:T(8,128)(2,1)S(1)}, bf16[1024,128]{1,0:T(8,128)(2,1)S(1)}, u32[]{:S(2)}, u32[]{:S(2)}) collective-permute-start(bf16[1024,128]{1,0:T(8,128)(2,1)S(1)} %get-tuple-element.57), channel_id=1, source_target_pairs={{0,6},{1,7},{2,0},{3,1},{4,2},{5,3},{6,4},{7,5},{8,14},{9,15},{10,... | collective-permute-start | bytes 786440 | tf_op jit(solution)/shard_map/ppermute | solution.py:392
  157.7 17.0 %collective-permute-start.6 = (bf16[1024,128]{1,0:T(8,128)(2,1)S(1)}, bf16[1024,128]{1,0:T(8,128)(2,1)S(1)}, u32[]{:S(2)}, u32[]{:S(2)}) collective-permute-start(bf16[1024,128]{1,0:T(8,128)(2,1)S(1)} %copy-done.12), channel_id=1, source_target_pairs={{0,7},{1,6},{2,1},{3,0},{4,3},{5,2},{6,5},{7,4},{8,15},{9,14},{10,... | collective-permute-start | bytes 786440 | tf_op jit(solution)/shard_map/ppermute | solution.py:392
  174.7 0.7 copy-start.9
  181.9 41.4 %all-to-all-start.5 = ((bf16[16,512,128]{2,1,0:T(8,128)(2,1)}), bf16[16,512,128]{2,1,0:T(8,128)(2,1)}, u32[]{:S(2)}, u32[]{:S(2)}) async-start(bf16[16,512,128]{2,1,0:T(8,128)(2,1)} %bitcast.83), calls=%async_computation.5 | async-start | bytes 4194304 | tf_op jit(solution)/shard_map/all_to_all | solution.py:352
  202.0 21.2 %copy-start.1 = (bf16[1024,512]{1,0:T(8,128)(2,1)S(1)}, bf16[1024,512]{1,0:T(8,128)(2,1)}, u32[]{:S(2)}) copy-start(bf16[1024,512]{1,0:T(8,128)(2,1)} %constant.59.clone.refs_2_) | copy-start | bytes 3145732

commit v2 on v1

--- a/solution.py
+++ b/solution.py
@@ -95,14 +95,18 @@
 
 
 def lookup_kernel(ids_ref, vol_ref, out_ref, tmp_ref):
-    def peer(p, carry):
-        at = pl.multiple_of(p * (2 * CAP), 8)
-        for s in range(CAP):
-            block = jnp.maximum(ids_ref[p, s], 0)
-            tmp_ref[pl.ds(at + 2 * s, 2), :] = vol_ref[pl.ds(pl.multiple_of(2 * block, 2), 2), :]
+    unroll = 4
+
+    def peers(i, carry):
+        at = pl.multiple_of(i * (2 * CAP * unroll), 8)
+        for j in range(unroll):
+            for s in range(CAP):
+                block = jnp.maximum(ids_ref[i * unroll + j, s], 0)
+                row = vol_ref[pl.ds(pl.multiple_of(2 * block, 2), 2), :]
+                tmp_ref[pl.ds(at + 2 * (CAP * j + s), 2), :] = row
         return carry
 
-    lax.fori_loop(0, ids_ref.shape[0], peer, 0)
+    lax.fori_loop(0, ids_ref.shape[0] // unroll, peers, 0)
     out_ref[...] = tmp_ref[...].astype(BF)
 
 
@@ -274,7 +278,7 @@
         out_specs=(whole,) * 2,
         compiler_params=params(),
         name="slots",
-    )(own, bid)
+    )(*[pltpu.with_memory_space_constraint(x, pltpu.HBM) for x in (own, bid)])
     got = lax.all_to_all(
         sent.reshape(peers, 1, 128), ("gx", "gy"), split_axis=0, concat_axis=0, tiled=True
     ).reshape(peers, 128)

time: 234 us -> 232 us (level)
    unnamed x30 -> x26, local copies, waits for them, and re-layouts: 9.03 us -> 7.67 us
where the time goes in v2:
time: 232 us; the launch traced here: 231 us
  waiting for transfers between devices  83.3 us (36%)
  Pallas kernels  64.5 us (28%)
  starting transfers between devices  45.4 us (20%)
  local copies, waits for them, and re-layouts  20.5 us (9%)
  other arithmetic  12.6 us (5%)
  between operations  4.52 us (2%)
    ppermute x7, waiting for transfers between devices, local(): arrived.append(lax.ppermute(pieces[k], 'gy', pairs))  20.5 us
    all_to_all x2, waiting for transfers between devices, cross(): lax.all_to_all(x, 'gx', split_axis=0, concat_axis=0, tiled=True)  17 us
    all_to_all x1, waiting for transfers between devices, local(): lax.all_to_all(outgoing.reshape(peers, 2 * CAP, block_len), ('gx', 'gy'),...  16.5 us
    all_to_all x1, waiting for transfers between devices, local(): arrived = lax.all_to_all(out, 'gy', split_axis=0, concat_axis=0, tiled=True)  13.3 us
    all_to_all x1, waiting for transfers between devices, local(): lax.all_to_all(looked.reshape(peers, 2 * CAP, block_len), ('gx', 'gy'), s...  13.3 us
    pallas_call x1, Pallas kernels, local(): pl.pallas_call(lambda *r, first_line=start * local_b: insert_next(first_l...  12.2 us
    pallas_call x1, Pallas kernels, local(): pl.pallas_call(insert_first, grid=(steps,), out_shape=(update_shape, jax....  11.8 us
    all_to_all x2, starting transfers between devices, cross(): lax.all_to_all(x, 'gx', split_axis=0, concat_axis=0, tiled=True)  11.7 us
  transfers between devices with their start and end apart: 13, of which 8 were waited for; matrix products, arithmetic and copies ran while one was open for 13% of the time, Pallas kernels for 10%

profile of v2, /device:TPU:0, one launch (start us, length us, event | category | flops | bytes accessed | tf_op | source)
XLA Modules:
  0.0 230.8 jit_solution(15372912370275321339)
XLA Ops:
  0.6 2.0 slots.1
  2.7 11.1 %all-to-all-start = ((s32[128,1,128]{2,1,0:T(1,128)}), s32[128,1,128]{2,1,0:T(1,128)S(1)}, u32[]{:S(2)}, u32[]{:S(2)}) async-start(s32[128,1,128]{2,1,0:T(1,128)} %bitcast.5), calls=%async_computation | async-start | bytes 131072 | tf_op jit(solution)/shard_map/all_to_all | solution.py:282
  13.8 6.6 %convert.7 = f32[2048,2,4,128]{3,1,2,0:T(2,128)} convert(bf16[2048,2,4,128]{3,1,2,0:T(2,128)(2,1)} %bitcast.78) | non-fusion elementwise | flops 2097152 | bytes 12582912 | tf_op jit(solution)/shard_map/reshape | solution.py:293
  20.4 2.6 %all-to-all-done = s32[128,1,128]{2,1,0:T(1,128)S(1)} async-done(((s32[128,1,128]{2,1,0:T(1,128)}), s32[128,1,128]{2,1,0:T(1,128)S(1)}, u32[]{:S(2)}, u32[]{:S(2)}) %all-to-all-start) | async-done | bytes 65568 | tf_op jit(solution)/shard_map/all_to_all | solution.py:282
  23.1 8.8 %lookup.1 = bf16[5120,128]{1,0:T(8,128)(2,1)} custom-call(s32[128,128]{1,0:T(8,128)S(1)} %bitcast.66, f32[16384,128]{1,0:T(8,128)} %bitcast.77), custom_call_target="tpu_custom_call" | custom-call | tf_op jit(solution)/shard_map/lookup/pallas_call | solution.py:295
  31.9 7.1 %all-to-all-start.1 = ((bf16[128,40,128]{2,1,0:T(8,128)(2,1)}), bf16[128,40,128]{2,1,0:T(8,128)(2,1)S(1)}, u32[]{:S(2)}, u32[]{:S(2)}) async-start(bf16[128,40,128]{2,1,0:T(8,128)(2,1)} %bitcast.10), calls=%async_computation.1 | async-start | bytes 2621440 | tf_op jit(solution)/shard_map/all_to_all | solution.py:304
  40.3 0.1 copy.26
  40.5 0.6 fusion.9
  41.7 0.1 select_reduce_fusion
  41.9 0.6 fusion.11
  42.5 1.2 sine_negate_fusion.ctf_ref
  43.7 0.4 fusion.10
  44.1 2.6 %fusion = (f32[512,128]{1,0:T(8,128)S(1)}, f32[512,128]{1,0:T(8,128)S(1)}) fusion(f32[]{:T(128)} %bitcast.17, f32[]{:T(128)} %bitcast.16, bf16[1,512,1,128]{3,2,1,0:T(2,128)(2,1)S(1)} %get-tuple-element.64, bf16[1,512,1,128]{3,2,1,0:T(2,128)(2,1)S(1)} %get-tuple-element.63), kind=kLoop, calls=%fused_computation.12 | loop fusion | flops 2686976 | bytes 786440 | tf_op jit(solution)/shard_map/sub | solution.py:318
  46.7 0.8 pad_maximum_fusion.shift_ref
  47.5 0.1 reshape.144.id_ref.r_2_
  47.6 13.3 %all-to-all-done.1 = bf16[128,40,128]{2,1,0:T(8,128)(2,1)S(1)} async-done(((bf16[128,40,128]{2,1,0:T(8,128)(2,1)}), bf16[128,40,128]{2,1,0:T(8,128)(2,1)S(1)}, u32[]{:S(2)}, u32[]{:S(2)}) %all-to-all-start.1) | async-done | bytes 1310752 | tf_op jit(solution)/shard_map/all_to_all | solution.py:304
  60.9 5.6 %particle.1 = (bf16[5120,128]{1,0:T(8,128)(2,1)}, f32[1,256]{1,0:T(1,128)S(1)}) custom-call(s32[1,1024]{1,0:T(1,128)S(1)} %get-tuple-element.32.target_ref.row_ref, bf16[5120,128]{1,0:T(8,128)(2,1)S(1)} %bitcast.64, s32[1,1024]{1,0:T(1,128)S(1)} %get-tuple-element.32.target_ref.row_ref, f32[512,2]{1,0:T(8,128)S(1)} %bitcast.65, ...), custom_call_target="tpu_custom_call" | custom-call | tf_op jit(solution)/shard_map/particle/pallas_call | solution.py:325
  66.5 4.6 %all-to-all-start.2 = ((bf16[128,40,128]{2,1,0:T(8,128)(2,1)}), bf16[128,40,128]{2,1,0:T(8,128)(2,1)S(1)}, u32[]{:S(2)}, u32[]{:S(2)}) async-start(bf16[128,40,128]{2,1,0:T(8,128)(2,1)} %bitcast.83), calls=%async_computation.2 | async-start | bytes 2621440 | tf_op jit(solution)/shard_map/all_to_all | solution.py:337
  71.2 5.4 %copy.31 = bf16[256,8,2,512]{3,1,2,0:T(8,128)(2,1)} copy(bf16[256,8,2,512]{3,2,1,0:T(2,128)(2,1)} %bitcast.79) | data formatting | bytes 8388608
  76.6 16.5 %all-to-all-done.2 = bf16[128,40,128]{2,1,0:T(8,128)(2,1)S(1)} async-done(((bf16[128,40,128]{2,1,0:T(8,128)(2,1)}), bf16[128,40,128]{2,1,0:T(8,128)(2,1)S(1)}, u32[]{:S(2)}, u32[]{:S(2)}) %all-to-all-start.2) | async-done | bytes 1310752 | tf_op jit(solution)/shard_map/all_to_all | solution.py:337
  93.1 11.8 %insert0.1 = (f32[2048,1024]{1,0:T(8,128)}, bf16[8,1024,128]{2,1,0:T(8,128)(2,1)}) custom-call(bf16[5120,128]{1,0:T(8,128)(2,1)S(1)} %bitcast.61, s32[1,2560]{1,0:T(1,128)S(1)} %reshape.144.id_ref.r_2_, bf16[2048,1024]{1,0:T(8,128)(2,1)} %bitcast.75, bf16[1024,1024]{1,0:T(8,128)(2,1)} %constant.57.clone.table_ref.r_4_), custom_call_target="tpu_custom_call" | custom-call | tf_op jit(solution)/shard_map/insert0/pallas_call | solution.py:369
  104.9 3.8 %all-to-all-start.3 = ((bf16[8,1024,128]{2,1,0:T(8,128)(2,1)}), bf16[8,1024,128]{2,1,0:T(8,128)(2,1)S(1)}, u32[]{:S(2)}, u32[]{:S(2)}) async-start(bf16[8,1024,128]{2,1,0:T(8,128)(2,1)} %get-tuple-element.40), calls=%async_computation.3 | async-start | bytes 4194304 | tf_op jit(solution)/shard_map/all_to_all | solution.py:379
  108.7 12.2 %insert1.1 = (f32[2048,1024]{1,0:T(8,128)}, bf16[1024,128]{1,0:T(8,128)(2,1)S(1)}, bf16[1024,128]{1,0:T(8,128)(2,1)S(1)}, bf16[1024,128]{1,0:T(8,128)(2,1)S(1)},...) custom-call(s32[1]{0:T(128)} %bitcast.24.r_0_.iy_ref, ...), custom_call_target="tpu_custom_call", output_to_operand_aliasing={{0}: (5, {})} | custom-call | tf_op jit(solution)/shard_map/insert1/pallas_call | solution.py:381
  120.9 0.7 copy-done.2
  121.6 0.7 copy-done.4
  122.3 13.3 %all-to-all-done.3 = bf16[8,1024,128]{2,1,0:T(8,128)(2,1)S(1)} async-done(((bf16[8,1024,128]{2,1,0:T(8,128)(2,1)}), bf16[8,1024,128]{2,1,0:T(8,128)(2,1)S(1)}, u32[]{:S(2)}, u32[]{:S(2)}) %all-to-all-start.3) | async-done | bytes 2097184 | tf_op jit(solution)/shard_map/all_to_all | solution.py:379
  135.6 5.9 %second0.1 = bf16[8192,128]{1,0:T(8,128)(2,1)} custom-call(bf16[8,16,64,128]{3,2,1,0:T(8,128)(2,1)S(1)} %bitcast.63, bf16[512,1024]{1,0:T(8,128)(2,1)} %constant.58.clone.table_ref.refs_8_), custom_call_target="tpu_custom_call" | custom-call | tf_op jit(solution)/shard_map/second0/pallas_call | solution.py:406
  141.5 4.6 %all-to-all-start.4 = ((bf16[16,512,128]{2,1,0:T(8,128)(2,1)}), bf16[16,512,128]{2,1,0:T(8,128)(2,1)}, u32[]{:S(2)}, u32[]{:S(2)}) async-start(bf16[16,512,128]{2,1,0:T(8,128)(2,1)} %bitcast.80), calls=%async_computation.4 | async-start | bytes 4194304 | tf_op jit(solution)/shard_map/all_to_all | solution.py:356
  146.1 0.1 collective-permute-start
  146.2 0.7 collective-permute-start.1
  146.8 0.1 collective-permute-start.2
  146.9 3.8 %collective-permute-start.3 = (bf16[1024,128]{1,0:T(8,128)(2,1)S(1)}, bf16[1024,128]{1,0:T(8,128)(2,1)S(1)}, u32[]{:S(2)}, u32[]{:S(2)}) collective-permute-start(bf16[1024,128]{1,0:T(8,128)(2,1)S(1)} %get-tuple-element.55), channel_id=1, source_target_pairs={{0,4},{1,5},{2,6},{3,7},{4,0},{5,1},{6,2},{7,3},{8,12},{9,13},{10,... | collective-permute-start | bytes 786440 | tf_op jit(solution)/shard_map/ppermute | solution.py:396
  150.7 0.0 collective-permute-start.4
  150.7 0.0 collective-permute-done
  150.7 2.3 %collective-permute-start.5 = (bf16[1024,128]{1,0:T(8,128)(2,1)S(1)}, bf16[1024,128]{1,0:T(8,128)(2,1)S(1)}, u32[]{:S(2)}, u32[]{:S(2)}) collective-permute-start(bf16[1024,128]{1,0:T(8,128)(2,1)S(1)} %get-tuple-element.57), channel_id=1, source_target_pairs={{0,6},{1,7},{2,0},{3,1},{4,2},{5,3},{6,4},{7,5},{8,14},{9,15},{10,... | collective-permute-start | bytes 786440 | tf_op jit(solution)/shard_map/ppermute | solution.py:396
  153.0 3.5 %collective-permute-done.1 = bf16[1024,128]{1,0:T(8,128)(2,1)S(1)} collective-permute-done((bf16[1024,128]{1,0:T(8,128)(2,1)S(1)}, bf16[1024,128]{1,0:T(8,128)(2,1)S(1)}, u32[]{:S(2)}, u32[]{:S(2)}) %collective-permute-start.1) | collective-permute-done | bytes 262176 | tf_op jit(solution)/shard_map/ppermute | solution.py:396
  156.6 0.0 collective-permute-start.6
  156.6 15.9 %collective-permute-done.2 = bf16[1024,128]{1,0:T(8,128)(2,1)S(1)} collective-permute-done((bf16[1024,128]{1,0:T(8,128)(2,1)S(1)}, bf16[1024,128]{1,0:T(8,128)(2,1)S(1)}, u32[]{:S(2)}, u32[]{:S(2)}) %collective-permute-start.2) | collective-permute-done | bytes 262176 | tf_op jit(solution)/shard_map/ppermute | solution.py:396
  172.5 1.1 collective-permute-done.6
  173.6 0.7 copy-done.7
  174.3 6.4 %second1.1 = bf16[8192,128]{1,0:T(8,128)(2,1)} custom-call(s32[1]{0:T(128)} %bitcast.24.r_0_.iy_ref, bf16[16,64,128]{2,1,0:T(8,128)(2,1)S(1)} %bitcast.68, bf16[16,64,128]{2,1,0:T(8,128)(2,1)S(1)} %bitcast.69, bf16[16,64,128]{2,1,0:T(8,128)(2,1)S(1)} %bitcast.70, bf16[16,64,128]{2,1,0:T(8,128)(2,1)S(1)} %bitcast.71, bf16[16,64,128]{2,1,0:T(8,128)(2,1)S(1)} %bitcast.72, ...), custom_call_target="tpu_custom_call" | custom-call | tf_op jit(solution)/shard_map/second1/pallas_call | solution.py:414
  180.7 0.0 all-to-all-done.4
  180.7 7.2 %all-to-all-start.5 = ((bf16[16,512,128]{2,1,0:T(8,128)(2,1)}), bf16[16,512,128]{2,1,0:T(8,128)(2,1)}, u32[]{:S(2)}, u32[]{:S(2)}) async-start(bf16[16,512,128]{2,1,0:T(8,128)(2,1)} %bitcast.81), calls=%async_computation.5 | async-start | bytes 4194304 | tf_op jit(solution)/shard_map/all_to_all | solution.py:356
  187.9 0.6 reduce_sum.32
  189.1 11.7 %reshape.166 = f32[32,64,2,512]{3,2,1,0:T(2,128)} reshape(f32[2048,1024]{1,0:T(8,128)} %get-tuple-element.59) | data formatting | bytes 16777216 | tf_op jit(solution)/shard_map/reshape | solution.py:454
  200.8 4.2 %turn0.1.refs_0_ = bf16[32,128,256]{2,1,0:T(8,128)(2,1)} custom-call(bf16[16,32,16,128]{3,2,1,0:T(8,128)(2,1)} %bitcast.27.in_ref), custom_call_target="tpu_custom_call" | custom-call | tf_op jit(solution)/shard_map/turn0/pallas_call | solution.py:434
  205.1 17.0 %all-to-all-done.5 = bf16[16,512,128]{2,1,0:T(8,128)(2,1)} async-done(((bf16[16,512,128]{2,1,0:T(8,128)(2,1)}), bf16[16,512,128]{2,1,0:T(8,128)(2,1)}, u32[]{:S(2)}, u32[]{:S(2)}) %all-to-all-start.5) | async-done | bytes 2097184 | tf_op jit(solution)/shard_map/all_to_all | solution.py:356
  222.0 7.6 %first.1 = bf16[32,2,64,512]{3,2,1,0:T(8,128)(2,1)} custom-call(bf16[32,128,256]{2,1,0:T(8,128)(2,1)} %turn0.1.refs_0_, bf16[16,32,16,128]{3,2,1,0:T(8,128)(2,1)} %bitcast.37.refs_1_, bf16[1024,512]{1,0:T(8,128)(2,1)S(1)} %copy-done.1), custom_call_target="tpu_custom_call" | custom-call | tf_op jit(solution)/shard_map/first/pallas_call | solution.py:445
  (25 shorter events, 0.1 us)
Async XLA Ops:
  2.7 20.4 %all-to-all-start = ((s32[128,1,128]{2,1,0:T(1,128)}), s32[128,1,128]{2,1,0:T(1,128)S(1)}, u32[]{:S(2)}, u32[]{:S(2)}) async-start(s32[128,1,128]{2,1,0:T(1,128)} %bitcast.5), calls=%async_computation | async-start | bytes 131072 | tf_op jit(solution)/shard_map/all_to_all | solution.py:282
  31.8 8.5 %copy-start.8 = (f32[1,512,2]{1,2,0:T(2,128)S(1)}, f32[1,512,2]{1,2,0:T(2,128)}, u32[]{:S(2)}) copy-start(f32[1,512,2]{1,2,0:T(2,128)} %param.14) | copy-start | bytes 12292
  31.8 8.6 %copy-start.11 = (f32[16]{0:T(128)S(1)}, f32[16]{0:T(128)}, u32[]{:S(2)}) copy-start(f32[16]{0:T(128)} %param.20) | copy-start | bytes 196
  31.8 9.9 %copy-start.9 = (f32[64,2]{0,1:T(2,128)S(1)}, f32[64,2]{0,1:T(2,128)}, u32[]{:S(2)}) copy-start(f32[64,2]{0,1:T(2,128)} %param.19) | copy-start | bytes 1540
  31.9 11.8 %copy-start.6 = (bf16[1,512,2,128]{3,2,1,0:T(2,128)(2,1)S(1)}, bf16[1,512,2,128]{3,2,1,0:T(2,128)(2,1)}, u32[]{:S(2)}) copy-start(bf16[1,512,2,128]{3,2,1,0:T(2,128)(2,1)} %param.13) | copy-start | bytes 786436
  31.9 29.1 %all-to-all-start.1 = ((bf16[128,40,128]{2,1,0:T(8,128)(2,1)}), bf16[128,40,128]{2,1,0:T(8,128)(2,1)S(1)}, u32[]{:S(2)}, u32[]{:S(2)}) async-start(bf16[128,40,128]{2,1,0:T(8,128)(2,1)} %bitcast.10), calls=%async_computation.1 | async-start | bytes 2621440 | tf_op jit(solution)/shard_map/all_to_all | solution.py:304
  66.5 26.6 %all-to-all-start.2 = ((bf16[128,40,128]{2,1,0:T(8,128)(2,1)}), bf16[128,40,128]{2,1,0:T(8,128)(2,1)S(1)}, u32[]{:S(2)}, u32[]{:S(2)}) async-start(bf16[128,40,128]{2,1,0:T(8,128)(2,1)} %bitcast.83), calls=%async_computation.2 | async-start | bytes 2621440 | tf_op jit(solution)/shard_map/all_to_all | solution.py:337
  93.1 11.8 %copy-start = (bf16[128,40,128]{2,1,0:T(8,128)(2,1)}, bf16[128,40,128]{2,1,0:T(8,128)(2,1)S(1)}, u32[]{:S(2)}) copy-start(bf16[128,40,128]{2,1,0:T(8,128)(2,1)S(1)} %all-to-all-done.2) | copy-start | bytes 3932164
  104.9 30.7 %all-to-all-start.3 = ((bf16[8,1024,128]{2,1,0:T(8,128)(2,1)}), bf16[8,1024,128]{2,1,0:T(8,128)(2,1)S(1)}, u32[]{:S(2)}, u32[]{:S(2)}) async-start(bf16[8,1024,128]{2,1,0:T(8,128)(2,1)} %get-tuple-element.40), calls=%async_computation.3 | async-start | bytes 4194304 | tf_op jit(solution)/shard_map/all_to_all | solution.py:379
  120.9 0.7 copy-start.2
  121.6 0.7 copy-start.4
  141.5 4.6 %copy-start.5 = (bf16[1024,128]{1,0:T(8,128)(2,1)S(1)}, bf16[1024,128]{1,0:T(8,128)(2,1)}, u32[]{:S(2)}) copy-start(bf16[1024,128]{1,0:T(8,128)(2,1)} %copy-done.4) | copy-start | bytes 786436
  141.5 4.7 %copy-start.3 = (bf16[1024,128]{1,0:T(8,128)(2,1)S(1)}, bf16[1024,128]{1,0:T(8,128)(2,1)}, u32[]{:S(2)}) copy-start(bf16[1024,128]{1,0:T(8,128)(2,1)} %copy-done.2) | copy-start | bytes 786436
  141.5 15.1 %copy-start.10 = (bf16[1024,128]{1,0:T(8,128)(2,1)S(1)}, bf16[1024,128]{1,0:T(8,128)(2,1)}, u32[]{:S(2)}) copy-start(bf16[1024,128]{1,0:T(8,128)(2,1)} %get-tuple-element.58) | copy-start | bytes 786436
  141.5 39.2 %all-to-all-start.4 = ((bf16[16,512,128]{2,1,0:T(8,128)(2,1)}), bf16[16,512,128]{2,1,0:T(8,128)(2,1)}, u32[]{:S(2)}, u32[]{:S(2)}) async-start(bf16[16,512,128]{2,1,0:T(8,128)(2,1)} %bitcast.80), calls=%async_computation.4 | async-start | bytes 4194304 | tf_op jit(solution)/shard_map/all_to_all | solution.py:356
  146.1 4.7 %collective-permute-start = (bf16[1024,128]{1,0:T(8,128)(2,1)S(1)}, bf16[1024,128]{1,0:T(8,128)(2,1)S(1)}, u32[]{:S(2)}, u32[]{:S(2)}) collective-permute-start(bf16[1024,128]{1,0:T(8,128)(2,1)S(1)} %copy-done.5), channel_id=1, source_target_pairs={{0,1},{1,0},{2,3},{3,2},{4,5},{5,4},{6,7},{7,6},{8,9},{9,8},{10,11... | collective-permute-start | bytes 786440 | tf_op jit(solution)/shard_map/ppermute | solution.py:396
  146.2 10.4 %collective-permute-start.1 = (bf16[1024,128]{1,0:T(8,128)(2,1)S(1)}, bf16[1024,128]{1,0:T(8,128)(2,1)S(1)}, u32[]{:S(2)}, u32[]{:S(2)}) collective-permute-start(bf16[1024,128]{1,0:T(8,128)(2,1)S(1)} %copy-done.3), channel_id=1, source_target_pairs={{0,2},{1,3},{2,4},{3,5},{4,6},{5,7},{6,0},{7,1},{8,10},{9,11},{10,... | collective-permute-start | bytes 786440 | tf_op jit(solution)/shard_map/ppermute | solution.py:396
  146.8 25.7 %collective-permute-start.2 = (bf16[1024,128]{1,0:T(8,128)(2,1)S(1)}, bf16[1024,128]{1,0:T(8,128)(2,1)S(1)}, u32[]{:S(2)}, u32[]{:S(2)}) collective-permute-start(bf16[1024,128]{1,0:T(8,128)(2,1)S(1)} %get-tuple-element.54), channel_id=1, source_target_pairs={{0,3},{1,2},{2,5},{3,4},{4,7},{5,6},{6,1},{7,0},{8,11},{9,10},{10,... | collective-permute-start | bytes 786440 | tf_op jit(solution)/shard_map/ppermute | solution.py:396
  146.9 25.6 %collective-permute-start.3 = (bf16[1024,128]{1,0:T(8,128)(2,1)S(1)}, bf16[1024,128]{1,0:T(8,128)(2,1)S(1)}, u32[]{:S(2)}, u32[]{:S(2)}) collective-permute-start(bf16[1024,128]{1,0:T(8,128)(2,1)S(1)} %get-tuple-element.55), channel_id=1, source_target_pairs={{0,4},{1,5},{2,6},{3,7},{4,0},{5,1},{6,2},{7,3},{8,12},{9,13},{10,... | collective-permute-start | bytes 786440 | tf_op jit(solution)/shard_map/ppermute | solution.py:396
  150.7 21.8 %collective-permute-start.4 = (bf16[1024,128]{1,0:T(8,128)(2,1)S(1)}, bf16[1024,128]{1,0:T(8,128)(2,1)S(1)}, u32[]{:S(2)}, u32[]{:S(2)}) collective-permute-start(bf16[1024,128]{1,0:T(8,128)(2,1)S(1)} %get-tuple-element.56), channel_id=1, source_target_pairs={{0,5},{1,4},{2,7},{3,6},{4,1},{5,0},{6,3},{7,2},{8,13},{9,12},{10,... | collective-permute-start | bytes 786440 | tf_op jit(solution)/shard_map/ppermute | solution.py:396
  150.7 21.8 %collective-permute-start.5 = (bf16[1024,128]{1,0:T(8,128)(2,1)S(1)}, bf16[1024,128]{1,0:T(8,128)(2,1)S(1)}, u32[]{:S(2)}, u32[]{:S(2)}) collective-permute-start(bf16[1024,128]{1,0:T(8,128)(2,1)S(1)} %get-tuple-element.57), channel_id=1, source_target_pairs={{0,6},{1,7},{2,0},{3,1},{4,2},{5,3},{6,4},{7,5},{8,14},{9,15},{10,... | collective-permute-start | bytes 786440 | tf_op jit(solution)/shard_map/ppermute | solution.py:396
  156.6 17.0 %collective-permute-start.6 = (bf16[1024,128]{1,0:T(8,128)(2,1)S(1)}, bf16[1024,128]{1,0:T(8,128)(2,1)S(1)}, u32[]{:S(2)}, u32[]{:S(2)}) collective-permute-start(bf16[1024,128]{1,0:T(8,128)(2,1)S(1)} %copy-done.10), channel_id=1, source_target_pairs={{0,7},{1,6},{2,1},{3,0},{4,3},{5,2},{6,5},{7,4},{8,15},{9,14},{10,... | collective-permute-start | bytes 786440 | tf_op jit(solution)/shard_map/ppermute | solution.py:396
  173.6 0.7 copy-start.7
  180.7 41.3 %all-to-all-start.5 = ((bf16[16,512,128]{2,1,0:T(8,128)(2,1)}), bf16[16,512,128]{2,1,0:T(8,128)(2,1)}, u32[]{:S(2)}, u32[]{:S(2)}) async-start(bf16[16,512,128]{2,1,0:T(8,128)(2,1)} %bitcast.81), calls=%async_computation.5 | async-start | bytes 4194304 | tf_op jit(solution)/shard_map/all_to_all | solution.py:356
  200.8 21.2 %copy-start.1 = (bf16[1024,512]{1,0:T(8,128)(2,1)S(1)}, bf16[1024,512]{1,0:T(8,128)(2,1)}, u32[]{:S(2)}) copy-start(bf16[1024,512]{1,0:T(8,128)(2,1)} %constant.59.clone.refs_2_) | copy-start | bytes 3145732

commit v3 on v2

--- a/solution.py
+++ b/solution.py
@@ -69,7 +69,9 @@
 
 def shifted_index(iy, k, gy, direction):
     chips = gy // 2
-    return ((iy // 2 + chips + direction * (k // 2)) % chips) * 2 + (iy % 2 + k % 2) % 2
+    later = sorted(range(1, gy), key=lambda i: (i // 2 not in (1, chips - 1), i // 2 == 0, i % 2))
+    far, core = divmod(([0] + later)[k], 2)
+    return ((iy // 2 + chips + direction * far) % chips) * 2 + (iy % 2 + core) % 2
 
 
 def slots_kernel(own_ref, bid_ref, sent_ref, row_ref):

time: 232 us -> 231 us (level)
  transfers between devices with their start and end apart: 13 -> 13, of which waited for: 8 -> 8; matrix products, arithmetic and copies ran while one was open for 13% -> 14% of each run, Pallas kernels for 10% -> 10%
where the time goes in v3:
time: 231 us; the launch traced here: 229 us
  waiting for transfers between devices  82.3 us (36%)
  Pallas kernels  64.5 us (28%)
  starting transfers between devices  44.5 us (19%)
  local copies, waits for them, and re-layouts  20.5 us (9%)
  other arithmetic  12.6 us (5%)
  between operations  4.52 us (2%)
    ppermute x7, waiting for transfers between devices, local(): arrived.append(lax.ppermute(pieces[k], 'gy', pairs))  18.9 us
    all_to_all x2, waiting for transfers between devices, cross(): lax.all_to_all(x, 'gx', split_axis=0, concat_axis=0, tiled=True)  17.6 us
    all_to_all x1, waiting for transfers between devices, local(): lax.all_to_all(outgoing.reshape(peers, 2 * CAP, block_len), ('gx', 'gy'),...  16.5 us
    all_to_all x1, waiting for transfers between devices, local(): arrived = lax.all_to_all(out, 'gy', split_axis=0, concat_axis=0, tiled=True)  13.4 us
    all_to_all x1, waiting for transfers between devices, local(): lax.all_to_all(looked.reshape(peers, 2 * CAP, block_len), ('gx', 'gy'), s...  13.3 us
    pallas_call x1, Pallas kernels, local(): pl.pallas_call(lambda *r, first_line=start * local_b: insert_next(first_l...  12.2 us
    pallas_call x1, Pallas kernels, local(): pl.pallas_call(insert_first, grid=(steps,), out_shape=(update_shape, jax....  11.7 us
    reshape x1, local copies, waits for them, and re-layouts, local(): update = update.reshape(local_a, local_b, 2, length)  11.7 us
  transfers between devices with their start and end apart: 13, of which 8 were waited for; matrix products, arithmetic and copies ran while one was open for 14% of the time, Pallas kernels for 10%

profile of v3, /device:TPU:0, one launch (start us, length us, event | category | flops | bytes accessed | tf_op | source)
XLA Modules:
  0.0 228.9 jit_solution(17830761618347276134)
XLA Ops:
  0.6 2.0 slots.1
  2.7 11.1 %all-to-all-start = ((s32[128,1,128]{2,1,0:T(1,128)}), s32[128,1,128]{2,1,0:T(1,128)S(1)}, u32[]{:S(2)}, u32[]{:S(2)}) async-start(s32[128,1,128]{2,1,0:T(1,128)} %bitcast.5), calls=%async_computation | async-start | bytes 131072 | tf_op jit(solution)/shard_map/all_to_all | solution.py:284
  13.8 6.6 %convert.7 = f32[2048,2,4,128]{3,1,2,0:T(2,128)} convert(bf16[2048,2,4,128]{3,1,2,0:T(2,128)(2,1)} %bitcast.78) | non-fusion elementwise | flops 2097152 | bytes 12582912 | tf_op jit(solution)/shard_map/reshape | solution.py:295
  20.4 2.6 %all-to-all-done = s32[128,1,128]{2,1,0:T(1,128)S(1)} async-done(((s32[128,1,128]{2,1,0:T(1,128)}), s32[128,1,128]{2,1,0:T(1,128)S(1)}, u32[]{:S(2)}, u32[]{:S(2)}) %all-to-all-start) | async-done | bytes 65568 | tf_op jit(solution)/shard_map/all_to_all | solution.py:284
  23.1 8.8 %lookup.1 = bf16[5120,128]{1,0:T(8,128)(2,1)} custom-call(s32[128,128]{1,0:T(8,128)S(1)} %bitcast.66, f32[16384,128]{1,0:T(8,128)} %bitcast.77), custom_call_target="tpu_custom_call" | custom-call | tf_op jit(solution)/shard_map/lookup/pallas_call | solution.py:297
  31.9 7.1 %all-to-all-start.1 = ((bf16[128,40,128]{2,1,0:T(8,128)(2,1)}), bf16[128,40,128]{2,1,0:T(8,128)(2,1)S(1)}, u32[]{:S(2)}, u32[]{:S(2)}) async-start(bf16[128,40,128]{2,1,0:T(8,128)(2,1)} %bitcast.10), calls=%async_computation.1 | async-start | bytes 2621440 | tf_op jit(solution)/shard_map/all_to_all | solution.py:306
  40.3 0.1 copy.26
  40.5 0.6 fusion.9
  41.7 0.1 select_reduce_fusion
  41.9 0.6 fusion.11
  42.5 1.2 sine_negate_fusion.ctf_ref
  43.7 0.4 fusion.10
  44.1 2.6 %fusion = (f32[512,128]{1,0:T(8,128)S(1)}, f32[512,128]{1,0:T(8,128)S(1)}) fusion(f32[]{:T(128)} %bitcast.17, f32[]{:T(128)} %bitcast.16, bf16[1,512,1,128]{3,2,1,0:T(2,128)(2,1)S(1)} %get-tuple-element.64, bf16[1,512,1,128]{3,2,1,0:T(2,128)(2,1)S(1)} %get-tuple-element.63), kind=kLoop, calls=%fused_computation.12 | loop fusion | flops 2686976 | bytes 786440 | tf_op jit(solution)/shard_map/sub | solution.py:320
  46.7 0.8 pad_maximum_fusion.shift_ref
  47.5 0.1 reshape.144.id_ref.r_2_
  47.6 13.3 %all-to-all-done.1 = bf16[128,40,128]{2,1,0:T(8,128)(2,1)S(1)} async-done(((bf16[128,40,128]{2,1,0:T(8,128)(2,1)}), bf16[128,40,128]{2,1,0:T(8,128)(2,1)S(1)}, u32[]{:S(2)}, u32[]{:S(2)}) %all-to-all-start.1) | async-done | bytes 1310752 | tf_op jit(solution)/shard_map/all_to_all | solution.py:306
  60.9 5.6 %particle.1 = (bf16[5120,128]{1,0:T(8,128)(2,1)}, f32[1,256]{1,0:T(1,128)S(1)}) custom-call(s32[1,1024]{1,0:T(1,128)S(1)} %get-tuple-element.32.target_ref.row_ref, bf16[5120,128]{1,0:T(8,128)(2,1)S(1)} %bitcast.64, s32[1,1024]{1,0:T(1,128)S(1)} %get-tuple-element.32.target_ref.row_ref, f32[512,2]{1,0:T(8,128)S(1)} %bitcast.65, ...), custom_call_target="tpu_custom_call" | custom-call | tf_op jit(solution)/shard_map/particle/pallas_call | solution.py:327
  66.5 4.6 %all-to-all-start.2 = ((bf16[128,40,128]{2,1,0:T(8,128)(2,1)}), bf16[128,40,128]{2,1,0:T(8,128)(2,1)S(1)}, u32[]{:S(2)}, u32[]{:S(2)}) async-start(bf16[128,40,128]{2,1,0:T(8,128)(2,1)} %bitcast.83), calls=%async_computation.2 | async-start | bytes 2621440 | tf_op jit(solution)/shard_map/all_to_all | solution.py:339
  71.2 5.4 %copy.31 = bf16[256,8,2,512]{3,1,2,0:T(8,128)(2,1)} copy(bf16[256,8,2,512]{3,2,1,0:T(2,128)(2,1)} %bitcast.79) | data formatting | bytes 8388608
  76.6 16.5 %all-to-all-done.2 = bf16[128,40,128]{2,1,0:T(8,128)(2,1)S(1)} async-done(((bf16[128,40,128]{2,1,0:T(8,128)(2,1)}), bf16[128,40,128]{2,1,0:T(8,128)(2,1)S(1)}, u32[]{:S(2)}, u32[]{:S(2)}) %all-to-all-start.2) | async-done | bytes 1310752 | tf_op jit(solution)/shard_map/all_to_all | solution.py:339
  93.1 11.7 %insert0.1 = (f32[2048,1024]{1,0:T(8,128)}, bf16[8,1024,128]{2,1,0:T(8,128)(2,1)}) custom-call(bf16[5120,128]{1,0:T(8,128)(2,1)S(1)} %bitcast.61, s32[1,2560]{1,0:T(1,128)S(1)} %reshape.144.id_ref.r_2_, bf16[2048,1024]{1,0:T(8,128)(2,1)} %bitcast.75, bf16[1024,1024]{1,0:T(8,128)(2,1)} %constant.57.clone.table_ref.r_4_), custom_call_target="tpu_custom_call" | custom-call | tf_op jit(solution)/shard_map/insert0/pallas_call | solution.py:371
  104.8 3.8 %all-to-all-start.3 = ((bf16[8,1024,128]{2,1,0:T(8,128)(2,1)}), bf16[8,1024,128]{2,1,0:T(8,128)(2,1)S(1)}, u32[]{:S(2)}, u32[]{:S(2)}) async-start(bf16[8,1024,128]{2,1,0:T(8,128)(2,1)} %get-tuple-element.40), calls=%async_computation.3 | async-start | bytes 4194304 | tf_op jit(solution)/shard_map/all_to_all | solution.py:381
  108.6 12.2 %insert1.1 = (f32[2048,1024]{1,0:T(8,128)}, bf16[1024,128]{1,0:T(8,128)(2,1)S(1)}, bf16[1024,128]{1,0:T(8,128)(2,1)S(1)}, bf16[1024,128]{1,0:T(8,128)(2,1)S(1)},...) custom-call(s32[1]{0:T(128)} %bitcast.24.r_0_.iy_ref, ...), custom_call_target="tpu_custom_call", output_to_operand_aliasing={{0}: (5, {})} | custom-call | tf_op jit(solution)/shard_map/insert1/pallas_call | solution.py:383
  120.8 0.7 copy-done.2
  121.5 0.7 copy-done.4
  122.2 13.4 %all-to-all-done.3 = bf16[8,1024,128]{2,1,0:T(8,128)(2,1)S(1)} async-done(((bf16[8,1024,128]{2,1,0:T(8,128)(2,1)}), bf16[8,1024,128]{2,1,0:T(8,128)(2,1)S(1)}, u32[]{:S(2)}, u32[]{:S(2)}) %all-to-all-start.3) | async-done | bytes 2097184 | tf_op jit(solution)/shard_map/all_to_all | solution.py:381
  135.6 5.9 %second0.1 = bf16[8192,128]{1,0:T(8,128)(2,1)} custom-call(bf16[8,16,64,128]{3,2,1,0:T(8,128)(2,1)S(1)} %bitcast.63, bf16[512,1024]{1,0:T(8,128)(2,1)} %constant.58.clone.table_ref.refs_8_), custom_call_target="tpu_custom_call" | custom-call | tf_op jit(solution)/shard_map/second0/pallas_call | solution.py:408
  141.5 4.6 %all-to-all-start.4 = ((bf16[16,512,128]{2,1,0:T(8,128)(2,1)}), bf16[16,512,128]{2,1,0:T(8,128)(2,1)}, u32[]{:S(2)}, u32[]{:S(2)}) async-start(bf16[16,512,128]{2,1,0:T(8,128)(2,1)} %bitcast.80), calls=%async_computation.4 | async-start | bytes 4194304 | tf_op jit(solution)/shard_map/all_to_all | solution.py:358
  146.1 0.6 collective-permute-start
  146.7 2.7 %collective-permute-start.1 = (bf16[1024,128]{1,0:T(8,128)(2,1)S(1)}, bf16[1024,128]{1,0:T(8,128)(2,1)S(1)}, u32[]{:S(2)}, u32[]{:S(2)}) collective-permute-start(bf16[1024,128]{1,0:T(8,128)(2,1)S(1)} %copy-done.3), channel_id=1, source_target_pairs={{0,6},{1,7},{2,0},{3,1},{4,2},{5,3},{6,4},{7,5},{8,14},{9,15},{10,... | collective-permute-start | bytes 786440 | tf_op jit(solution)/shard_map/ppermute | solution.py:398
  149.4 0.0 collective-permute-start.2
  149.4 3.0 %collective-permute-start.3 = (bf16[1024,128]{1,0:T(8,128)(2,1)S(1)}, bf16[1024,128]{1,0:T(8,128)(2,1)S(1)}, u32[]{:S(2)}, u32[]{:S(2)}) collective-permute-start(bf16[1024,128]{1,0:T(8,128)(2,1)S(1)} %get-tuple-element.55), channel_id=1, source_target_pairs={{0,7},{1,6},{2,1},{3,0},{4,3},{5,2},{6,5},{7,4},{8,15},{9,14},{10,... | collective-permute-start | bytes 786440 | tf_op jit(solution)/shard_map/ppermute | solution.py:398
  152.3 4.2 %collective-permute-done = bf16[1024,128]{1,0:T(8,128)(2,1)S(1)} collective-permute-done((bf16[1024,128]{1,0:T(8,128)(2,1)S(1)}, bf16[1024,128]{1,0:T(8,128)(2,1)S(1)}, u32[]{:S(2)}, u32[]{:S(2)}) %collective-permute-start) | collective-permute-done | bytes 262176 | tf_op jit(solution)/shard_map/ppermute | solution.py:398
  156.6 0.0 collective-permute-start.5
  156.6 0.0 collective-permute-done.1
  156.6 0.1 collective-permute-start.6
  156.7 3.4 %collective-permute-done.2 = bf16[1024,128]{1,0:T(8,128)(2,1)S(1)} collective-permute-done((bf16[1024,128]{1,0:T(8,128)(2,1)S(1)}, bf16[1024,128]{1,0:T(8,128)(2,1)S(1)}, u32[]{:S(2)}, u32[]{:S(2)}) %collective-permute-start.2) | collective-permute-done | bytes 262176 | tf_op jit(solution)/shard_map/ppermute | solution.py:398
  160.1 11.2 %collective-permute-done.3 = bf16[1024,128]{1,0:T(8,128)(2,1)S(1)} collective-permute-done((bf16[1024,128]{1,0:T(8,128)(2,1)S(1)}, bf16[1024,128]{1,0:T(8,128)(2,1)S(1)}, u32[]{:S(2)}, u32[]{:S(2)}) %collective-permute-start.3) | collective-permute-done | bytes 262176 | tf_op jit(solution)/shard_map/ppermute | solution.py:398
  171.3 0.0 collective-permute-done.4
  171.4 0.0 copy-start.7
  171.4 0.7 copy-done.7
  172.1 6.4 %second1.1 = bf16[8192,128]{1,0:T(8,128)(2,1)} custom-call(s32[1]{0:T(128)} %bitcast.24.r_0_.iy_ref, bf16[16,64,128]{2,1,0:T(8,128)(2,1)S(1)} %bitcast.68, bf16[16,64,128]{2,1,0:T(8,128)(2,1)S(1)} %bitcast.69, bf16[16,64,128]{2,1,0:T(8,128)(2,1)S(1)} %bitcast.70, bf16[16,64,128]{2,1,0:T(8,128)(2,1)S(1)} %bitcast.71, bf16[16,64,128]{2,1,0:T(8,128)(2,1)S(1)} %bitcast.72, ...), custom_call_target="tpu_custom_call" | custom-call | tf_op jit(solution)/shard_map/second1/pallas_call | solution.py:416
  178.5 6.9 %all-to-all-start.5 = ((bf16[16,512,128]{2,1,0:T(8,128)(2,1)}), bf16[16,512,128]{2,1,0:T(8,128)(2,1)}, u32[]{:S(2)}, u32[]{:S(2)}) async-start(bf16[16,512,128]{2,1,0:T(8,128)(2,1)} %bitcast.81), calls=%async_computation.5 | async-start | bytes 4194304 | tf_op jit(solution)/shard_map/all_to_all | solution.py:358
  185.4 0.6 reduce_sum.32
  186.6 11.7 %reshape.166 = f32[32,64,2,512]{3,2,1,0:T(2,128)} reshape(f32[2048,1024]{1,0:T(8,128)} %get-tuple-element.59) | data formatting | bytes 16777216 | tf_op jit(solution)/shard_map/reshape | solution.py:456
  198.3 4.2 %turn0.1.refs_0_ = bf16[32,128,256]{2,1,0:T(8,128)(2,1)} custom-call(bf16[16,32,16,128]{3,2,1,0:T(8,128)(2,1)} %bitcast.27.in_ref), custom_call_target="tpu_custom_call" | custom-call | tf_op jit(solution)/shard_map/turn0/pallas_call | solution.py:436
  202.6 17.6 %all-to-all-done.5 = bf16[16,512,128]{2,1,0:T(8,128)(2,1)} async-done(((bf16[16,512,128]{2,1,0:T(8,128)(2,1)}), bf16[16,512,128]{2,1,0:T(8,128)(2,1)}, u32[]{:S(2)}, u32[]{:S(2)}) %all-to-all-start.5) | async-done | bytes 2097184 | tf_op jit(solution)/shard_map/all_to_all | solution.py:358
  220.2 7.6 %first.1 = bf16[32,2,64,512]{3,2,1,0:T(8,128)(2,1)} custom-call(bf16[32,128,256]{2,1,0:T(8,128)(2,1)} %turn0.1.refs_0_, bf16[16,32,16,128]{3,2,1,0:T(8,128)(2,1)} %bitcast.37.refs_1_, bf16[1024,512]{1,0:T(8,128)(2,1)S(1)} %copy-done.1), custom_call_target="tpu_custom_call" | custom-call | tf_op jit(solution)/shard_map/first/pallas_call | solution.py:447
  (25 shorter events, 0.1 us)
Async XLA Ops:
  2.7 20.4 %all-to-all-start = ((s32[128,1,128]{2,1,0:T(1,128)}), s32[128,1,128]{2,1,0:T(1,128)S(1)}, u32[]{:S(2)}, u32[]{:S(2)}) async-start(s32[128,1,128]{2,1,0:T(1,128)} %bitcast.5), calls=%async_computation | async-start | bytes 131072 | tf_op jit(solution)/shard_map/all_to_all | solution.py:284
  31.8 8.5 %copy-start.8 = (f32[1,512,2]{1,2,0:T(2,128)S(1)}, f32[1,512,2]{1,2,0:T(2,128)}, u32[]{:S(2)}) copy-start(f32[1,512,2]{1,2,0:T(2,128)} %param.14) | copy-start | bytes 12292
  31.8 8.6 %copy-start.11 = (f32[16]{0:T(128)S(1)}, f32[16]{0:T(128)}, u32[]{:S(2)}) copy-start(f32[16]{0:T(128)} %param.20) | copy-start | bytes 196
  31.8 9.9 %copy-start.9 = (f32[64,2]{0,1:T(2,128)S(1)}, f32[64,2]{0,1:T(2,128)}, u32[]{:S(2)}) copy-start(f32[64,2]{0,1:T(2,128)} %param.19) | copy-start | bytes 1540
  31.9 11.8 %copy-start.6 = (bf16[1,512,2,128]{3,2,1,0:T(2,128)(2,1)S(1)}, bf16[1,512,2,128]{3,2,1,0:T(2,128)(2,1)}, u32[]{:S(2)}) copy-start(bf16[1,512,2,128]{3,2,1,0:T(2,128)(2,1)} %param.13) | copy-start | bytes 786436
  31.9 29.1 %all-to-all-start.1 = ((bf16[128,40,128]{2,1,0:T(8,128)(2,1)}), bf16[128,40,128]{2,1,0:T(8,128)(2,1)S(1)}, u32[]{:S(2)}, u32[]{:S(2)}) async-start(bf16[128,40,128]{2,1,0:T(8,128)(2,1)} %bitcast.10), calls=%async_computation.1 | async-start | bytes 2621440 | tf_op jit(solution)/shard_map/all_to_all | solution.py:306
  66.5 26.6 %all-to-all-start.2 = ((bf16[128,40,128]{2,1,0:T(8,128)(2,1)}), bf16[128,40,128]{2,1,0:T(8,128)(2,1)S(1)}, u32[]{:S(2)}, u32[]{:S(2)}) async-start(bf16[128,40,128]{2,1,0:T(8,128)(2,1)} %bitcast.83), calls=%async_computation.2 | async-start | bytes 2621440 | tf_op jit(solution)/shard_map/all_to_all | solution.py:339
  93.1 11.7 %copy-start = (bf16[128,40,128]{2,1,0:T(8,128)(2,1)}, bf16[128,40,128]{2,1,0:T(8,128)(2,1)S(1)}, u32[]{:S(2)}) copy-start(bf16[128,40,128]{2,1,0:T(8,128)(2,1)S(1)} %all-to-all-done.2) | copy-start | bytes 3932164
  104.8 30.7 %all-to-all-start.3 = ((bf16[8,1024,128]{2,1,0:T(8,128)(2,1)}), bf16[8,1024,128]{2,1,0:T(8,128)(2,1)S(1)}, u32[]{:S(2)}, u32[]{:S(2)}) async-start(bf16[8,1024,128]{2,1,0:T(8,128)(2,1)} %get-tuple-element.40), calls=%async_computation.3 | async-start | bytes 4194304 | tf_op jit(solution)/shard_map/all_to_all | solution.py:381
  120.8 0.7 copy-start.2
  121.5 0.7 copy-start.4
  141.5 4.6 %copy-start.5 = (bf16[1024,128]{1,0:T(8,128)(2,1)S(1)}, bf16[1024,128]{1,0:T(8,128)(2,1)}, u32[]{:S(2)}) copy-start(bf16[1024,128]{1,0:T(8,128)(2,1)} %copy-done.4) | copy-start | bytes 786436
  141.5 5.2 %copy-start.3 = (bf16[1024,128]{1,0:T(8,128)(2,1)S(1)}, bf16[1024,128]{1,0:T(8,128)(2,1)}, u32[]{:S(2)}) copy-start(bf16[1024,128]{1,0:T(8,128)(2,1)} %copy-done.2) | copy-start | bytes 786436
  141.5 15.1 %copy-start.10 = (bf16[1024,128]{1,0:T(8,128)(2,1)S(1)}, bf16[1024,128]{1,0:T(8,128)(2,1)}, u32[]{:S(2)}) copy-start(bf16[1024,128]{1,0:T(8,128)(2,1)} %get-tuple-element.58) | copy-start | bytes 786436
  141.5 37.0 %all-to-all-start.4 = ((bf16[16,512,128]{2,1,0:T(8,128)(2,1)}), bf16[16,512,128]{2,1,0:T(8,128)(2,1)}, u32[]{:S(2)}, u32[]{:S(2)}) async-start(bf16[16,512,128]{2,1,0:T(8,128)(2,1)} %bitcast.80), calls=%async_computation.4 | async-start | bytes 4194304 | tf_op jit(solution)/shard_map/all_to_all | solution.py:358
  146.1 10.5 %collective-permute-start = (bf16[1024,128]{1,0:T(8,128)(2,1)S(1)}, bf16[1024,128]{1,0:T(8,128)(2,1)S(1)}, u32[]{:S(2)}, u32[]{:S(2)}) collective-permute-start(bf16[1024,128]{1,0:T(8,128)(2,1)S(1)} %copy-done.5), channel_id=1, source_target_pairs={{0,2},{1,3},{2,4},{3,5},{4,6},{5,7},{6,0},{7,1},{8,10},{9,11},{10,... | collective-permute-start | bytes 786440 | tf_op jit(solution)/shard_map/ppermute | solution.py:398
  146.7 9.9 %collective-permute-start.1 = (bf16[1024,128]{1,0:T(8,128)(2,1)S(1)}, bf16[1024,128]{1,0:T(8,128)(2,1)S(1)}, u32[]{:S(2)}, u32[]{:S(2)}) collective-permute-start(bf16[1024,128]{1,0:T(8,128)(2,1)S(1)} %copy-done.3), channel_id=1, source_target_pairs={{0,6},{1,7},{2,0},{3,1},{4,2},{5,3},{6,4},{7,5},{8,14},{9,15},{10,... | collective-permute-start | bytes 786440 | tf_op jit(solution)/shard_map/ppermute | solution.py:398
  149.4 10.7 %collective-permute-start.2 = (bf16[1024,128]{1,0:T(8,128)(2,1)S(1)}, bf16[1024,128]{1,0:T(8,128)(2,1)S(1)}, u32[]{:S(2)}, u32[]{:S(2)}) collective-permute-start(bf16[1024,128]{1,0:T(8,128)(2,1)S(1)} %get-tuple-element.54), channel_id=1, source_target_pairs={{0,3},{1,2},{2,5},{3,4},{4,7},{5,6},{6,1},{7,0},{8,11},{9,10},{10,... | collective-permute-start | bytes 786440 | tf_op jit(solution)/shard_map/ppermute | solution.py:398
  149.4 22.0 %collective-permute-start.3 = (bf16[1024,128]{1,0:T(8,128)(2,1)S(1)}, bf16[1024,128]{1,0:T(8,128)(2,1)S(1)}, u32[]{:S(2)}, u32[]{:S(2)}) collective-permute-start(bf16[1024,128]{1,0:T(8,128)(2,1)S(1)} %get-tuple-element.55), channel_id=1, source_target_pairs={{0,7},{1,6},{2,1},{3,0},{4,3},{5,2},{6,5},{7,4},{8,15},{9,14},{10,... | collective-permute-start | bytes 786440 | tf_op jit(solution)/shard_map/ppermute | solution.py:398
  152.3 19.0 %collective-permute-start.4 = (bf16[1024,128]{1,0:T(8,128)(2,1)S(1)}, bf16[1024,128]{1,0:T(8,128)(2,1)S(1)}, u32[]{:S(2)}, u32[]{:S(2)}) collective-permute-start(bf16[1024,128]{1,0:T(8,128)(2,1)S(1)} %get-tuple-element.56), channel_id=1, source_target_pairs={{0,4},{1,5},{2,6},{3,7},{4,0},{5,1},{6,2},{7,3},{8,12},{9,13},{10,... | collective-permute-start | bytes 786440 | tf_op jit(solution)/shard_map/ppermute | solution.py:398
  156.6 14.8 %collective-permute-start.5 = (bf16[1024,128]{1,0:T(8,128)(2,1)S(1)}, bf16[1024,128]{1,0:T(8,128)(2,1)S(1)}, u32[]{:S(2)}, u32[]{:S(2)}) collective-permute-start(bf16[1024,128]{1,0:T(8,128)(2,1)S(1)} %get-tuple-element.57), channel_id=1, source_target_pairs={{0,5},{1,4},{2,7},{3,6},{4,1},{5,0},{6,3},{7,2},{8,13},{9,12},{10,... | collective-permute-start | bytes 786440 | tf_op jit(solution)/shard_map/ppermute | solution.py:398
  156.6 14.8 %collective-permute-start.6 = (bf16[1024,128]{1,0:T(8,128)(2,1)S(1)}, bf16[1024,128]{1,0:T(8,128)(2,1)S(1)}, u32[]{:S(2)}, u32[]{:S(2)}) collective-permute-start(bf16[1024,128]{1,0:T(8,128)(2,1)S(1)} %copy-done.10), channel_id=1, source_target_pairs={{0,1},{1,0},{2,3},{3,2},{4,5},{5,4},{6,7},{7,6},{8,9},{9,8},{10,11... | collective-permute-start | bytes 786440 | tf_op jit(solution)/shard_map/ppermute | solution.py:398
  171.4 0.7 copy-start.7
  178.5 41.7 %all-to-all-start.5 = ((bf16[16,512,128]{2,1,0:T(8,128)(2,1)}), bf16[16,512,128]{2,1,0:T(8,128)(2,1)}, u32[]{:S(2)}, u32[]{:S(2)}) async-start(bf16[16,512,128]{2,1,0:T(8,128)(2,1)} %bitcast.81), calls=%async_computation.5 | async-start | bytes 4194304 | tf_op jit(solution)/shard_map/all_to_all | solution.py:358
  198.3 21.8 %copy-start.1 = (bf16[1024,512]{1,0:T(8,128)(2,1)S(1)}, bf16[1024,512]{1,0:T(8,128)(2,1)}, u32[]{:S(2)}) copy-start(bf16[1024,512]{1,0:T(8,128)(2,1)} %constant.59.clone.refs_2_) | copy-start | bytes 3145732
